TPU v7x, 512 devices: a whole 4x8x8 slice. The times are simulated.
512 devices in a mesh: domain: 64 (over z_hi, x, y), band: 8 (over z_lo, core).
Axes of the slice: x: 4, y: 8, z: 8 (z_hi: 2, z_lo: 4; z = z_hi * 4 + z_lo), core: 2. Of those that a mesh axis runs over, the one named last changes fastest.
Arguments:
- start_block: bfloat16 [64896, 1024], P('domain', 'band'), may hold values from -2700 to 2700
- resident: bfloat16 [64896, 1024], P('domain', 'band'), may hold values from -16 to 16
- cell_kernel: bfloat16 [343, 343], replicated, may hold values from -0.3054414 to 3.3054414, as said below
- cell_scale: float32 [256], P('domain'), may hold values from 0.5 to 2
- potential: float32 [64896], P('domain'), may hold values from 0 to 4
- cell_nodes: int32 [256, 343], P('domain'), may hold values from 0 to 1182, as said below
- send_rows: int32 [10816], P('domain'), may hold values from 0 to 1013, as said below
Outputs:
- filtered_block: bfloat16 [64896, 1024], P('domain', 'band')
- margin: float32 [1024, 1024], P('domain', 'band')
Inputs may be any that keep to these rules, and one draw needn't show every extreme that they name: `cell_nodes`: cell c of slab s is a hexahedron of 7 by 7 by 7 nodes, node k = (kz * 7 + ky) * 7 + kx; the slab's cells form a 2 by 2 layer, neighbours share their faces' nodes; values below 1014 are the slab's own rows, value 1014 + j is the j-th entry of the next slab's send_rows (its node kz = 6 plane). `send_rows`: slab s's 169 entries are distinct rows of that slab, its nodes with kz = 0, in the order in which the slab below numbers them. `cell_kernel`: symmetric.
All inputs are finite; a program needn't handle non-finite values.
Results may differ from a plain program's by a relative error of at most 0.0033.
Values may be sent and summed in bfloat16 or wider, within the bound.
A program may use at most 64 MiB of HBM per device.

v0:
```python
import jax
import jax.numpy as jnp
from jax import lax
from jax.sharding import PartitionSpec as P

DEGREE = 8


lower_edge = 0.0
cutoff_edge = 16.0
upper_edge = 96.0
epsilon = 1e-06


def passed_along(array, axis, by):
    length = lax.axis_size(axis)
    pairs = [(i, i + by) for i in range(length) if 0 <= i + by < length]
    return lax.ppermute(array, axis, pairs)


def chebyshev_terms(degree):
    half_width = (upper_edge - cutoff_edge) / 2.0
    centre = (upper_edge + cutoff_edge) / 2.0
    sigma_now = half_width / (lower_edge - centre)
    gamma_ratio = 2.0 / sigma_now
    lead_factor = sigma_now / half_width
    recurrence = []
    for _ in range(degree - 1):
        sigma_next = 1.0 / (gamma_ratio - sigma_now)
        recurrence.append((2.0 * sigma_next / half_width, sigma_now * sigma_next))
        sigma_now = sigma_next
    return (centre, lead_factor, recurrence)


def per_device(start_block, resident, cell_kernel, cell_scale, potential, cell_nodes, send_rows):
    owned_rows = start_block.shape[0]
    plane_size = send_rows.shape[0]
    orbital_count = start_block.shape[1]
    cell_count = cell_nodes.shape[0]
    node_count = cell_kernel.shape[0]
    index_map = cell_nodes.T
    centre, lead_factor, recurrence = chebyshev_terms(DEGREE)

    def cell_sums(extended_low):
        cell_block = extended_low[index_map].reshape(node_count, cell_count * orbital_count)
        products = jnp.dot(cell_kernel, cell_block, preferred_element_type=jnp.float32)
        products = (
            products.reshape(node_count, cell_count, orbital_count) * cell_scale[None, :, None]
        )
        summed = jnp.zeros((owned_rows + plane_size, orbital_count), jnp.float32)
        return summed.at[index_map].add(products)

    def apply_ham(vector):
        rounded = vector.astype(jnp.bfloat16)
        ghost_rows = passed_along(rounded[send_rows], "domain", -1)
        summed = cell_sums(jnp.concatenate([rounded, ghost_rows], 0))
        returned = passed_along(summed[owned_rows:].astype(jnp.bfloat16), "domain", 1).astype(
            jnp.float32
        )
        return summed[:owned_rows].at[send_rows].add(returned) + potential[:, None] * vector

    former = start_block.astype(jnp.float32)
    current = lead_factor * (apply_ham(former) - centre * former)
    for lead_coeff, tail_coeff in recurrence:
        following = lead_coeff * (apply_ham(current) - centre * current) - tail_coeff * former
        former = current
        current = following
    squares = jnp.sum(current * current, 0)
    filtered_low = current.astype(jnp.bfloat16)
    contract_rows = (((0,), (0,)), ((), ()))
    partial_sums = lax.dot_general(
        lax.all_gather(resident, "band", axis=1, tiled=True),
        filtered_low,
        contract_rows,
        preferred_element_type=jnp.float32,
    )
    margin_local = lax.psum_scatter(partial_sums, "domain", scatter_dimension=0, tiled=True)
    column_total = lax.psum(squares, "domain")
    inverse = lax.rsqrt(column_total + epsilon)
    filtered_block = (current * inverse[None, :]).astype(jnp.bfloat16)
    return (filtered_block, margin_local * inverse[None, :])


def solution(mesh):
    return jax.shard_map(
        per_device,
        mesh=mesh,
        in_specs=(
            P("domain", "band"),
            P("domain", "band"),
            P(),
            P("domain"),
            P("domain"),
            P("domain", None),
            P("domain"),
        ),
        out_specs=(P("domain", "band"), P("domain", "band")),
        check_vma=False,
    )
```

profile of v0, /device:TPU:128, one launch (start us, length us, event | category | flops | bytes accessed | tf_op | source)
XLA Modules:
  0.0 753.2 jit_solution(9536676813056836660)
XLA Ops:
  7.9 1.7 gather_fusion
  9.6 1.3 collective-permute-start
  11.9 3.6 collective-permute-done
  15.5 1.0 pad_maximum_fusion
  16.5 3.3 gather_fusion.1
  21.2 9.1 %scatter_custom_fusion = f32[1183,128]{1,0:T(8,128)S(1)} fusion(s32[1372]{0:T(1024)S(1)} %reshape.313, f32[1372,128]{1,0:T(8,128)S(1)} %reshape.203, f32[]{:T(128)} %constant.22.clone.1), kind=kCustom, calls=%fused_computation.93 | custom fusion | flops 175616 | bytes 605700 | tf_op jit(solution)/shard_map/scatter-add | solution.py:51
  30.3 3.5 collective-permute-start.1
  34.1 1.5 collective-permute-done.1
  35.5 1.7 scatter_custom_fusion.1
  38.1 1.3 collective-permute-start.2
  39.4 4.9 collective-permute-done.2
  44.3 3.3 gather_fusion.3
  48.9 9.1 %scatter_custom_fusion.2 = f32[1183,128]{1,0:T(8,128)S(1)} fusion(s32[1372]{0:T(1024)S(1)} %reshape.313, f32[1372,128]{1,0:T(8,128)S(1)} %reshape.219, f32[]{:T(128)} %constant.22.clone.1), kind=kCustom, calls=%fused_computation.91 | custom fusion | flops 175616 | bytes 605700 | tf_op jit(solution)/shard_map/scatter-add | solution.py:51
  58.1 3.9 collective-permute-start.3
  62.3 1.4 collective-permute-done.3
  63.7 1.7 scatter_custom_fusion.3
  65.6 0.8 gather_fusion.4
  66.3 1.7 collective-permute-start.4
  68.1 4.5 collective-permute-done.4
  72.6 3.3 gather_fusion.5
  77.2 9.1 %scatter_custom_fusion.4 = f32[1183,128]{1,0:T(8,128)S(1)} fusion(s32[1372]{0:T(1024)S(1)} %reshape.313, f32[1372,128]{1,0:T(8,128)S(1)} %reshape.235, f32[]{:T(128)} %constant.22.clone.1), kind=kCustom, calls=%fused_computation.89 | custom fusion | flops 175616 | bytes 605700 | tf_op jit(solution)/shard_map/scatter-add | solution.py:51
  86.4 5.1 collective-permute-start.5
  91.7 1.5 collective-permute-done.5
  93.2 1.7 scatter_custom_fusion.5
  95.8 1.3 collective-permute-start.6
  97.1 5.0 collective-permute-done.6
  102.1 3.3 gather_fusion.7
  106.7 9.1 %scatter_custom_fusion.6 = f32[1183,128]{1,0:T(8,128)S(1)} fusion(s32[1372]{0:T(1024)S(1)} %reshape.313, f32[1372,128]{1,0:T(8,128)S(1)} %reshape.251, f32[]{:T(128)} %constant.22.clone.1), kind=kCustom, calls=%fused_computation.87 | custom fusion | flops 175616 | bytes 605700 | tf_op jit(solution)/shard_map/scatter-add | solution.py:51
  115.8 5.1 collective-permute-start.7
  121.2 1.5 collective-permute-done.7
  122.7 1.7 scatter_custom_fusion.7
  125.3 1.5 collective-permute-start.8
  126.7 4.8 collective-permute-done.8
  131.5 3.3 gather_fusion.9
  136.1 9.1 %scatter_custom_fusion.8 = f32[1183,128]{1,0:T(8,128)S(1)} fusion(s32[1372]{0:T(1024)S(1)} %reshape.313, f32[1372,128]{1,0:T(8,128)S(1)} %reshape.267, f32[]{:T(128)} %constant.22.clone.1), kind=kCustom, calls=%fused_computation.85 | custom fusion | flops 175616 | bytes 605700 | tf_op jit(solution)/shard_map/scatter-add | solution.py:51
  145.3 5.1 collective-permute-start.9
  150.6 1.5 collective-permute-done.9
  152.1 1.7 scatter_custom_fusion.9
  154.7 1.3 collective-permute-start.10
  156.1 4.9 collective-permute-done.10
  161.0 3.3 gather_fusion.11
  165.6 9.1 %scatter_custom_fusion.10 = f32[1183,128]{1,0:T(8,128)S(1)} fusion(s32[1372]{0:T(1024)S(1)} %reshape.313, f32[1372,128]{1,0:T(8,128)S(1)} %reshape.283, f32[]{:T(128)} %constant.22.clone.1), kind=kCustom, calls=%fused_computation.83 | custom fusion | flops 175616 | bytes 605700 | tf_op jit(solution)/shard_map/scatter-add | solution.py:51
  174.8 5.1 collective-permute-start.11
  180.1 1.5 collective-permute-done.11
  181.6 1.7 scatter_custom_fusion.11
  184.2 1.5 collective-permute-start.12
  185.7 4.7 collective-permute-done.12
  190.5 3.3 gather_fusion.13
  195.1 9.1 %scatter_custom_fusion.12 = f32[1183,128]{1,0:T(8,128)S(1)} fusion(s32[1372]{0:T(1024)S(1)} %reshape.313, f32[1372,128]{1,0:T(8,128)S(1)} %reshape.299, f32[]{:T(128)} %constant.22.clone.1), kind=kCustom, calls=%fused_computation.81 | custom fusion | flops 175616 | bytes 605700 | tf_op jit(solution)/shard_map/scatter-add | solution.py:51
  204.2 5.1 collective-permute-start.13
  209.6 1.5 collective-permute-done.13
  211.1 1.7 scatter_custom_fusion.13
  213.7 1.3 collective-permute-start.14
  215.0 5.0 collective-permute-done.14
  220.0 3.3 gather_fusion.15
  224.6 9.1 %scatter_custom_fusion.14 = f32[1183,128]{1,0:T(8,128)S(1)} fusion(s32[1372]{0:T(1024)S(1)} %reshape.313, f32[1372,128]{1,0:T(8,128)S(1)} %reshape.315, f32[]{:T(128)} %constant.22.clone.1), kind=kCustom, calls=%fused_computation.79 | custom fusion | flops 175616 | bytes 605700 | tf_op jit(solution)/shard_map/scatter-add | solution.py:51
  233.7 5.1 collective-permute-start.15
  239.0 1.5 collective-permute-done.15
  240.5 1.7 scatter_custom_fusion.15
  242.4 2.1 convolution_bitcast_fusion.8
  244.6 1.0 copy.14
  245.6 226.0 %psum.7 = f32[128]{0:T(128)S(1)} all-reduce(f32[128]{0:T(128)S(1)} %get-tuple-element.8), channel_id=1, replica_groups=mesh['domain'=64,'band'=8] {'domain'}, use_global_device_ids=true, to_apply=%region_17.0 | all-reduce | flops 128 | bytes 1024 | tf_op jit(solution)/shard_map/psum | solution.py:78
  472.4 272.2 %reduce-scatter.4.cloned.1.call-done = f32[16,128]{1,0:T(8,128)} async-done(((f32[1024,128]{1,0:T(8,128)}), f32[16,128]{1,0:T(8,128)}) %reduce-scatter.4.cloned.1.call-update) | async-done | bytes 8208
  744.6 0.8 copy.15
  (101 shorter events, 21.1 us)
Async XLA Ops:
  7.2 12.9 %copy-start = (bf16[343,343]{1,0:T(8,128)(2,1)S(1)}, bf16[343,343]{1,0:T(8,128)(2,1)}, u32[]{:S(2)}) copy-start(bf16[343,343]{1,0:T(8,128)(2,1)} %param.9) | copy-start | bytes 705898
  7.2 235.2 %all-gather.2.cloned.1.call-start = ((), (), s32[]{:S(2)}) async-start(), calls=%async_computation.1 | async-start | bytes 2340864 | tf_op jit(solution)/shard_map/all_gather | solution.py:72
  9.6 5.9 collective-permute-start
  19.9 0.9 copy-start.3
  20.7 13.1 %copy-start.1 = (bf16[1014,128]{1,0:T(8,128)(2,1)S(1)}, bf16[1014,128]{1,0:T(8,128)(2,1)}, u32[]{:S(2)}) copy-start(bf16[1014,128]{1,0:T(8,128)(2,1)} %param.7) | copy-start | bytes 778756
  20.7 13.1 %copy-start.2 = (f32[1014]{0:T(1024)S(1)}, f32[1014]{0:T(1024)}, u32[]{:S(2)}) copy-start(f32[1014]{0:T(1024)} %param.11) | copy-start | bytes 12172
  30.3 5.2 collective-permute-start.1
  38.1 6.2 collective-permute-start.2
  58.1 5.6 collective-permute-start.3
  66.3 6.2 collective-permute-start.4
  86.4 6.8 collective-permute-start.5
  95.8 6.3 collective-permute-start.6
  115.8 6.8 collective-permute-start.7
  125.3 6.2 collective-permute-start.8
  145.3 6.8 collective-permute-start.9
  154.7 6.2 collective-permute-start.10
  156.0 588.5 %reduce-scatter.4.cloned.1.call-start = ((), (), s32[]{:S(2)}) async-start(), calls=%async_computation.2 | async-start | bytes 532480
  174.8 6.8 collective-permute-start.11
  184.2 6.2 collective-permute-start.12
  204.2 6.8 collective-permute-start.13
  213.7 6.2 collective-permute-start.14
  233.7 6.8 collective-permute-start.15
Sparse Core Ops, SparseCore 0:
  156.2 77.0 all-gather.1
  245.7 498.8 reduce-scatter.3
where the time goes:
time: 763 us; the launch traced here: 753 us
  waiting for transfers between devices  321 us (42%)
  blocking collectives  226 us (30%)
  other arithmetic  94.2 us (12%)
  starting transfers between devices  49.4 us (6%)
  local copies, waits for them, and re-layouts  42.1 us (6%)
  between operations  15.2 us (2%)
    unnamed x3, waiting for transfers between devices  272 us
    psum x1, blocking collectives, per_device(): column_total = lax.psum(squares, 'domain')  226 us
    scatter-add x8, other arithmetic, cell_sums(): return summed.at[index_map].add(products)  72.9 us
    ppermute x16, starting transfers between devices, passed_along(): return lax.ppermute(array, axis, pairs)  49.3 us
    ppermute x16, waiting for transfers between devices, passed_along(): return lax.ppermute(array, axis, pairs)  49.2 us
    gather x8, local copies, waits for them, and re-layouts, cell_sums(): extended_low[index_map].reshape(node_count, cell_count * orbital_count)  26.6 us
  transfers between devices with their start and end apart: 18, of which 17 were waited for; matrix products, arithmetic and copies ran while one was open for 7% of the time, Pallas kernels for 0%

commit v1 on v0

v1 whole, which is shorter than its diff:
```python
import functools

import jax
import jax.numpy as jnp
from jax import lax
from jax.experimental import pallas as pl
from jax.experimental.pallas import tpu as pltpu
from jax.sharding import PartitionSpec as P

DEGREE = 8
EDGE = 7
ORB = 128
OWNED = 1014
PLANE = 169

lower_edge = 0.0
cutoff_edge = 16.0
upper_edge = 96.0
epsilon = 1e-06

NX = 13
XS = 112
NR = NX * XS
NRP = NR + 16
NRL = 1536
PL = 208
PLP = 256
MR = 392
KR = 448
KL = 384
OWNP = 1024

N_DOM = 64
N_ZH, N_X, N_Y = 2, 4, 8
N_ZL = 4

f32 = jnp.float32
bf16 = jnp.bfloat16
MESH = pl.DeviceIdType.MESH


def chebyshev_terms(degree):
    half_width = (upper_edge - cutoff_edge) / 2.0
    centre = (upper_edge + cutoff_edge) / 2.0
    sigma_now = half_width / (lower_edge - centre)
    gamma_ratio = 2.0 / sigma_now
    lead_factor = sigma_now / half_width
    recurrence = [(lead_factor, 0.0)]
    for _ in range(degree - 1):
        sigma_next = 1.0 / (gamma_ratio - sigma_now)
        recurrence.append((2.0 * sigma_next / half_width, sigma_now * sigma_next))
        sigma_now = sigma_next
    return (centre, recurrence)


CENTRE, TERMS = chebyshev_terms(DEGREE)


def mm(a, b):
    return jnp.dot(a, b, preferred_element_type=f32)


def mm_nt(a, b):
    return lax.dot_general(a, b, (((1,), (1,)), ((), ())), preferred_element_type=f32)


def mm_tn(a, b):
    return lax.dot_general(a, b, (((0,), (0,)), ((), ())), preferred_element_type=f32)


def iota(shape, dim):
    return lax.broadcasted_iota(jnp.int32, shape, dim)


def hot(cond):
    return jnp.where(cond, 1.0, 0.0).astype(bf16)


def pick(k, values):
    out = jnp.float32(values[0])
    for i in range(1, len(values)):
        out = jnp.where(k == i, jnp.float32(values[i]), out)
    return out


def kernel(
    start_ref, res_ref, ck_ref, scale_ref, pot_ref, cn_ref, cns_ref, sr_ref,
    out_ref, margin_ref,
    V, R, O, OG, part, potc, place, prow, Pm, PT, Q, st, kpad, K1, Kp, T, KgP, KttP, KgD,
    ET, F, W2, top_col, jbot_col, pot8, cnp, srp,
    Gs, cs, Gr, cr, Js, Jr, Us, Ur, RB, H2, LOW, CO, mpb, X1, M0, SF, SB, X2, N1s, N1r, N2s, N2r,
    g_send, g_recv, c_send, c_recv, j_sem, u_sem, r_send, r_recv, x1_send, x1_recv, x2_send, x2_recv,
    n1_send, n1_recv, n2_send, n2_recv,
):
    d = lax.axis_index("domain")
    band = lax.axis_index("band")
    zh = d // (N_X * N_Y)
    gx = (d // N_Y) % N_X
    gy = d % N_Y
    zl = band // 2
    core = band % 2
    sibling = zl * 2 + (1 - core)
    has_below = d > 0
    has_above = d < N_DOM - 1

    Gr[...] = jnp.zeros_like(Gr)
    cr[...] = jnp.zeros_like(cr)
    Jr[...] = jnp.full(Jr.shape, -3.0, f32)
    Ur[0:8, :] = jnp.full((8, PLP), -4.0, f32)
    Ur[8:16, :] = jnp.zeros((8, PLP), f32)

    barrier = pltpu.get_barrier_semaphore()

    def greet(dom, bnd):
        pl.semaphore_signal(barrier, inc=1, device_id=(dom, bnd), device_id_type=MESH)

    x_peers = [(zh * N_X + (gx + i) % N_X) * N_Y + gy for i in range(1, N_X)]
    x_from = x_peers
    yz_off = [(a, b) for a in range(N_ZH) for b in range(N_Y) if (a, b) != (0, 0)]
    yz_peers = [
        (((zh + a) % N_ZH) * N_X + gx) * N_Y + (gy + b) % N_Y for a, b in yz_off
    ]

    @pl.when(has_below)
    def _():
        greet(d - 1, band)

    @pl.when(has_above)
    def _():
        greet(d + 1, band)

    @pl.when(zl > 0)
    def _():
        greet(d, band - 2)

    @pl.when(zl < N_ZL - 1)
    def _():
        greet(d, band + 2)

    greet(d, sibling)
    for p in x_peers + yz_peers:
        greet(p, band)

    corner = [cns_ref[c, 0] for c in range(4)]
    right_x = [cns_ref[c, EDGE - 1] for c in range(4)]
    right_y = [cns_ref[c, EDGE * (EDGE - 1)] for c in range(4)]
    pos = []
    for c in range(4):
        in_x = sum([jnp.where(right_x[b] == corner[c], 1, 0) for b in range(4)])
        in_y = sum([jnp.where(right_y[b] == corner[c], 1, 0) for b in range(4)])
        pos.append(in_x + 2 * in_y)
    scale = []
    for p in range(4):
        s = jnp.float32(0.0)
        for c in range(4):
            s = s + jnp.where(pos[c] == p, scale_ref[c], 0.0)
        scale.append(s)

    cnp[...] = jnp.zeros_like(cnp)
    cnp[0:4, 0:343] = cn_ref[...]
    row8 = iota((8, KL), 0)
    full = jnp.zeros((8, KL), jnp.int32)
    for c in range(4):
        line = jnp.broadcast_to(cnp[c : c + 1, :], (8, KL))
        full = full + jnp.where((row8 & 3) == pos[c], line, 0)
    cn8 = jnp.where(row8 < 4, full >> 5, full & 31).astype(f32).astype(bf16)

    rr = iota((XS, KL), 0)
    ln = iota((XS, KL), 1)
    yy = rr >> 3
    zz = rr & 7
    k_base = jnp.where(
        (zz < EDGE) & (yy < NX), zz * 49 + jnp.where(yy > 6, yy - 6, yy) * 7, -1000
    )
    diff = k_base - ln
    l8 = iota((XS, 8), 1)
    y8 = iota((XS, 8), 0) >> 3
    z128 = iota((XS, 128), 0) & 7
    y128 = iota((XS, 128), 0) >> 3
    top_row = (z128 < EDGE) & (y128 < NX)
    own_row = (z128 < EDGE - 1) & (y128 < NX)
    weights = jnp.where(iota((8, 128), 0) < 4, 32.0, 1.0).astype(bf16)
    lane = iota((XS, 128), 1).astype(f32)
    for X in range(NX):
        x = X if X <= 6 else X - 6
        one = hot(diff == -x)
        Q[X * XS : (X + 1) * XS, :] = one
        a1 = mm_nt(one, cn8)
        cell = jnp.where(y8 > 6, 2, 0) + (1 if X > 6 else 0)
        a1 = jnp.where((l8 & 3) == cell, a1, 0.0).astype(bf16)
        pl_x = mm(a1, weights)
        place[X * XS : (X + 1) * XS, :] = jnp.where(top_row, pl_x, -1.0)
        own = jnp.where(own_row, pl_x, -1.0)
        for t in range(8):
            Pm[X * XS : (X + 1) * XS, t * 128 : (t + 1) * 128] = hot(own == lane + 128.0 * t)
    place[NR:NRP, :] = jnp.full((NRP - NR, 128), -1.0, f32)

    srp[...] = jnp.full(srp.shape, -5.0, f32)
    srp[0:1, 0:PLANE] = sr_ref[...].astype(f32)
    top_col[...] = jnp.full(top_col.shape, -1.0, f32)
    yrow = iota((16, 128), 0)
    lane16 = iota((16, 128), 1)
    ET[...] = jnp.zeros_like(ET)
    for X in range(NX):
        b0 = jnp.concatenate(
            [place[pl.ds(X * XS, 8, stride=8), :], place[pl.ds(X * XS + 64, 8, stride=8), :]], 0
        )
        b0 = jnp.where(yrow < NX, b0, -1.0)
        for t in range(2):
            ET[X * 16 : X * 16 + 16, t * 128 : (t + 1) * 128] = hot(
                b0 == srp[0:1, t * 128 : (t + 1) * 128]
            )
        t0 = jnp.concatenate(
            [place[pl.ds(X * XS + 6, 8, stride=8), :], place[pl.ds(X * XS + 70, 8, stride=8), :]],
            0,
        )
        top_col[X * 16 : X * 16 + 16, :] = jnp.where(yrow < NX, t0 - float(OWNED), -1.0)
    jm = iota((PLP, 128), 0).astype(f32).astype(bf16)
    p_row = iota((PLP, 128), 0)
    jb = mm(ET[...], jm)
    jbot_col[...] = jnp.where(((p_row & 15) < NX) & (p_row < PL), jb, -2.0)
    p_lane = iota((8, PLP), 1)
    p_ok = ((p_lane & 15) < NX) & (p_lane < PL)
    jr = mm_nt(iota((8, PLP), 1).astype(f32).astype(bf16), ET[...])
    Js[...] = jnp.where(p_ok, jr, -2.0)

    pr = iota((PLP, KL), 0)
    pln = iota((PLP, KL), 1)
    pX = pr >> 4
    pY = pr & 15
    p_in = (pX < NX) & (pY < NX)
    ox = jnp.where(pX > 6, pX - 6, pX)
    oy = jnp.where(pY > 6, pY - 6, pY)
    q_top = hot(p_in & (294 + oy * 7 + ox == pln))
    at = mm_nt(cn8, q_top)
    lX = p_lane >> 4
    lY = p_lane & 15
    l_cell = jnp.where(lX > 6, 1, 0) + jnp.where(lY > 6, 2, 0)
    r8 = iota((8, PLP), 0)
    at = jnp.where((r8 & 3) == l_cell, at, 0.0) * jnp.where(r8 < 4, 32.0, 1.0)
    top_line = jnp.sum(at, 0, keepdims=True) - float(OWNED)
    Us[0:8, :] = jnp.where(p_ok, jnp.broadcast_to(top_line, (8, PLP)), -1.0)
    srow = iota((8, PLP), 0)
    stile = jnp.zeros((8, PLP), f32)
    for c in range(4):
        stile = jnp.where(srow == c, scale[c], stile)
    Us[8:16, :] = stile

    RB[band, 1008:1024, :] = jnp.zeros((16, ORB), bf16)
    RB[band, 0:OWNED, :] = res_ref[...]

    ones = lambda cond: jnp.where(cond, 1, 0)
    count = (
        ones(has_below) + ones(has_above) + ones(zl > 0) + ones(zl < N_ZL - 1)
        + 1 + len(x_peers) + len(yz_peers)
    )
    pl.semaphore_wait(barrier, count)

    def remote(src, dst, ssem, rsem, dom, bnd):
        return pltpu.make_async_remote_copy(
            src_ref=src, dst_ref=dst, send_sem=ssem, recv_sem=rsem,
            device_id=(dom, bnd), device_id_type=MESH,
        )

    j_copy = remote(Js, Jr, j_sem.at[0], j_sem.at[1], d - 1, band)
    u_copy = remote(Us, Ur, u_sem.at[0], u_sem.at[1], d + 1, band)

    @pl.when(has_below)
    def _():
        j_copy.start()

    @pl.when(has_above)
    def _():
        u_copy.start()

    def block(src, to, s):
        return remote(RB.at[src], RB.at[src], r_send.at[s], r_recv.at[src], d, to)

    def send_own(start):
        def act(c):
            c.start() if start else c.wait_send()

        @pl.when(zl < N_ZL - 1)
        def _():
            act(block(band, band + 2, 0))

        @pl.when(zl > 0)
        def _():
            act(block(band, band - 2, 1))

        act(block(band, sibling, 2))

    def forward(dist, start):
        @pl.when(zl >= dist)
        def _():
            src = band - 2 * dist
            if start:
                block(src, sibling, 0).wait_recv()

            @pl.when(zl < N_ZL - 1)
            def _():
                c = block(src, band + 2, 3 * dist)
                c.start() if start else c.wait_send()

            c = block(src, sibling, 3 * dist + 1)
            c.start() if start else c.wait_send()

        @pl.when(zl + dist <= N_ZL - 1)
        def _():
            src = band + 2 * dist
            if start:
                block(src, sibling, 0).wait_recv()

            @pl.when(zl > 0)
            def _():
                c = block(src, band - 2, 9 + 3 * dist)
                c.start() if start else c.wait_send()

            c = block(src, sibling, 10 + 3 * dist)
            c.start() if start else c.wait_send()

    send_own(True)

    st[1008:1024, :] = jnp.zeros((16, ORB), bf16)
    st[0:OWNED, :] = start_ref[...]
    V[0, 0:NR, :] = mm(Pm[...], st[...])
    V[0, NR:NRP, :] = jnp.zeros((NRP - NR, ORB), f32)
    V[1, :, :] = jnp.zeros((NRP, ORB), f32)
    part[...] = jnp.zeros_like(part)
    zero8 = jnp.zeros((8, ORB), f32)
    for X in range(NX):
        R[X * 64 : X * 64 + 64, 0:128] = V[0, X * XS : X * XS + 64, :].astype(bf16)
        R[X * 64 : X * 64 + 64, 128:256] = V[0, X * XS + 48 : X * XS + 112, :].astype(bf16)

    kpad[...] = jnp.zeros_like(kpad)
    kpad[0:343, 0:343] = ck_ref[...]
    kmat = kpad[...]
    r56 = iota((56, KL), 0)
    k56 = jnp.where((r56 & 7) < 7, (r56 & 7) * 49 + (r56 >> 3) * 7, -1000) - iota((56, KL), 1)
    row_hot = jnp.concatenate([jnp.where(k56 == -x, 1.0, 0.0) for x in range(7)], 0).astype(bf16)
    r64 = iota((64, KL), 0)
    k64 = (
        jnp.where(((r64 & 7) < 7) & (r64 < 56), (r64 & 7) * 49 + (r64 >> 3) * 7, -1000)
        - iota((64, KL), 1)
    )
    col_hot = jnp.concatenate([hot(k64 == -x) for x in range(7)], 0)
    K1[...] = mm(row_hot, kmat).astype(bf16)
    Kp[...] = mm_nt(K1[...], col_hot).astype(bf16)
    r16 = iota((16, KL), 0)
    l16 = iota((16, KL), 1)
    for cy in range(2):
        y = r16 - 6 * cy
        kt = jnp.where((y >= 0) & (y < 7), 294 + y * 7, -1000) - l16
        t_hot = jnp.concatenate([hot(kt == -x) for x in range(7)], 0)
        T[cy] = mm_nt(mm(t_hot, kmat).astype(bf16), col_hot).astype(bf16)

    def down(k):
        return remote(
            Gs.at[k, pl.ds(0, PL)], Gr.at[k, pl.ds(0, PL)], g_send.at[k], g_recv.at[k], d - 1, band
        )

    def up(k):
        return remote(cs.at[k], cr.at[k, pl.ds(0, PL)], c_send.at[k], c_recv.at[k], d + 1, band)

    def send_planes(k, cur):
        Gs[k, PL:PLP, :] = jnp.zeros((PLP - PL, ORB), bf16)
        for X in range(NX):
            lo = V[cur, pl.ds(X * XS, 8, stride=8), :]
            hi = V[cur, pl.ds(X * XS + 64, 8, stride=8), :]
            Gs[k, X * 16 : X * 16 + 16, :] = jnp.concatenate([lo, hi], 0).astype(bf16)

        @pl.when(has_below)
        def _():
            down(k).start()

        c0 = mm(T[0], R[0:KR, 0:128]) * scale[0] + mm(T[1], R[0:KR, 128:256]) * scale[2]
        c1 = mm(T[0], R[384 : 384 + KR, 0:128]) * scale[1]
        c1 = c1 + mm(T[1], R[384 : 384 + KR, 128:256]) * scale[3]
        cs[k, 0:96, :] = c0[0:96].astype(bf16)
        cs[k, 96:112, :] = (c0[96:112] + c1[0:16]).astype(bf16)
        cs[k, 112:208, :] = c1[16:112].astype(bf16)

        @pl.when(has_above)
        def _():
            up(k).start()

    send_planes(0, 0)

    pot8[...] = jnp.zeros_like(pot8)
    pot = pot_ref[...]
    p_hi = pot.astype(bf16)
    rest = pot - p_hi.astype(f32)
    p_mid = rest.astype(bf16)
    p_lo = (rest - p_mid.astype(f32)).astype(bf16)
    pot8[0:1, 0:OWNED] = p_hi.astype(f32)
    pot8[1:2, 0:OWNED] = p_mid.astype(f32)
    pot8[2:3, 0:OWNED] = p_lo.astype(f32)
    pcol = mm_nt(Pm[...], pot8[...].astype(bf16)).astype(bf16)
    potc[...] = mm(pcol, jnp.ones((8, 128), bf16)) - CENTRE

    for c in range(4):
        cx, cy = c % 2, c // 2
        x = pX - 6 * cx
        y = pY - 6 * cy
        inside = (x >= 0) & (x < 7) & (y >= 0) & (y < 7)
        c_top = hot(inside & (294 + y * 7 + x == pln))
        KgP[c] = mm_nt(K1[...], c_top).astype(bf16)
        KttP[c] = mm_nt(mm(c_top, kmat).astype(bf16), c_top)

    lin = iota((8, NRL), 1)
    lin_x = jnp.floor((lin.astype(f32) + 0.5) * (1.0 / XS)).astype(jnp.int32)
    lin_r = lin - lin_x * XS
    lin_y = lin_r >> 3
    lin_z = lin_r & 7
    lin_cell = jnp.where(lin_x > 6, 1, 0) + jnp.where(lin_y > 6, 2, 0)
    lin_8 = iota((8, NRL), 0)
    Q[NR:NRL, :] = jnp.zeros((NRL - NR, KL), bf16)
    ar = mm_nt(cn8, Q[...])
    ar = jnp.where((lin_8 & 3) == lin_cell, ar, 0.0) * jnp.where(lin_8 < 4, 32.0, 1.0)
    ar = jnp.broadcast_to(jnp.sum(ar, 0, keepdims=True), (8, NRL))
    prow[...] = jnp.where((lin_x < NX) & (lin_y < NX) & (lin_z < EDGE - 1), ar, -1.0)
    n16 = iota((16, NRL), 0).astype(f32)

    def fill(i, carry):
        base = (i * 16).astype(f32)
        PT[pl.ds(pl.multiple_of(i * 16, 16), 16), :] = hot(prow[0:1, :] == n16 + base)
        return carry

    lax.fori_loop(0, OWNP // 16, fill, 0)

    @pl.when(has_above)
    def _():
        j_copy.wait_recv()

    @pl.when(has_below)
    def _():
        u_copy.wait_recv()

    tc = top_col[...]
    jc = jbot_col[...]
    m1 = jnp.concatenate([hot(tc == Jr[0:1, t * 128 : (t + 1) * 128]) for t in range(2)], 1)
    F[...] = jnp.concatenate([hot(jc == Ur[0:1, t * 128 : (t + 1) * 128]) for t in range(2)], 1)
    for c in range(4):
        KgD[c] = mm(KgP[c], m1).astype(bf16)
    w = jnp.zeros((PLP, PLP), f32)
    for c in range(4):
        w = w + KttP[c] * Ur[8 + c : 9 + c, :]
    w_hi = w.astype(bf16)
    w_lo = (w - w_hi.astype(f32)).astype(bf16)
    fm = F[...]
    W2[0] = mm_nt(mm(fm, w_hi).astype(bf16), fm).astype(bf16)
    W2[1] = mm_nt(mm(fm, w_lo).astype(bf16), fm).astype(bf16)

    mask8 = jnp.where(iota((8, ORB), 0) < EDGE - 1, 1.0, 0.0)

    def spread(ref_of, X, factor):
        lo, hi = None, None
        for cx in range(2):
            x = X - 6 * cx
            if 0 <= x < 7:
                a = ref_of(cx, 0, x).reshape(7, 8, ORB) * factor(cx, 0)
                b = ref_of(cx, 1, x).reshape(7, 8, ORB) * factor(cx, 1)
                lo = a if lo is None else lo + a
                hi = b if hi is None else hi + b
        return jnp.concatenate([lo[0:6], lo[6:7] + hi[0:1], hi[1:7]], 0)

    def bulk(k, cur):
        nxt = 1 - cur
        a = pick(k, [t[0] for t in TERMS])
        b = pick(k, [t[1] for t in TERMS])
        am = mask8 * a
        for cx in range(2):
            O[cx] = mm(Kp[...], R[384 * cx : 384 * cx + KR, :])
        for X in range(NX):
            rows = slice(X * XS, X * XS + 104)
            s = spread(
                lambda cx, cy, x: O[cx, x * 56 : x * 56 + 56, cy * 128 : (cy + 1) * 128],
                X,
                lambda cx, cy: scale[cx + 2 * cy],
            )
            v = V[cur, rows, :].reshape(NX, 8, ORB)
            u = V[nxt, rows, :].reshape(NX, 8, ORB)
            pc = potc[rows, :].reshape(NX, 8, ORB)
            new = (s + pc * v) * am[None] - b * u
            part[rows, :] = new.reshape(104, ORB)
        g = Gs[k]
        return (mm(W2[0], g) + mm(W2[1], g)) * a

    def finish(k, cur, plane, last):
        nxt = 1 - cur
        a = pick(k, [t[0] for t in TERMS])
        am = mask8 * a

        @pl.when(has_below)
        def _():
            up(k).wait_recv()

        e = plane + mm(F[...], cr[k]) * a
        for X in range(NX):
            lo = pl.ds(X * XS, 8, stride=8)
            hi = pl.ds(X * XS + 64, 8, stride=8)
            part[lo, :] = part[lo, :] + e[X * 16 : X * 16 + 8]
            part[hi, :] = part[hi, :] + e[X * 16 + 8 : X * 16 + 16]

        @pl.when(has_above)
        def _():
            down(k).wait_recv()

        for c in range(4):
            OG[c] = mm(KgD[c], Gr[k])
        sq = jnp.zeros((8, ORB), f32)
        for X in range(NX):
            rows = slice(X * XS, X * XS + 104)
            s = spread(
                lambda cx, cy, x: OG[cx + 2 * cy, x * 56 : x * 56 + 56, :],
                X,
                lambda cx, cy: (am * scale[cx + 2 * cy])[None],
            )
            new = part[rows, :].reshape(NX, 8, ORB) + s
            flat = new.reshape(104, ORB)
            if last:
                sq = sq + jnp.sum(new * new, 0)
                padded = jnp.concatenate([flat, zero8], 0)
                top = padded.astype(bf16)
                H2[X * XS : (X + 1) * XS, 0:128] = top
                H2[X * XS : (X + 1) * XS, 128:256] = (padded - top.astype(f32)).astype(bf16)
            else:
                V[nxt, rows, :] = flat
                R[X * 64 : X * 64 + 64, 0:128] = flat[0:64].astype(bf16)
                R[X * 64 : X * 64 + 64, 128:256] = jnp.concatenate(
                    [flat[48:104], zero8], 0
                ).astype(bf16)
        return sq

    def step(k, carry):
        cur = lax.rem(k, 2)
        plane = bulk(k, cur)

        @pl.when(k == 3)
        def _():
            forward(1, True)

        @pl.when(k == 5)
        def _():
            forward(2, True)

        finish(k, cur, plane, False)
        send_planes(k + 1, 1 - cur)
        return carry

    lax.fori_loop(0, DEGREE - 1, step, 0)
    final = DEGREE - 1
    plane = bulk(final, final % 2)
    forward(3, True)
    H2[NR:NRL, :] = jnp.zeros((NRL - NR, 256), bf16)
    sq = finish(final, final % 2, plane, True)

    N1s[...] = jnp.broadcast_to(jnp.sum(sq, 0, keepdims=True), (8, ORB))

    def n1(i):
        return remote(N1s, N1r.at[i], n1_send.at[i], n1_recv.at[i], x_peers[i], band)

    for i in range(3):
        n1(i).start()

    un = mm(PT[...], H2[...])
    LOW[...] = un[:, 0:128].astype(bf16)
    CO[...] = un[:, 0:128] + un[:, 128:256]

    for i in range(N_ZL):
        src = i * 2 + (1 - core)
        block(src, sibling, 0).wait_recv()

    def x1(i):
        return remote(mpb.at[i], X1.at[i], x1_send.at[i], x1_recv.at[i], x_peers[i], band)

    for i in range(4):
        tx = (gx + 1 + i) % N_X
        for h in range(N_ZH):
            m = mm_tn(RB[h * N_X + tx], LOW[...])
            if i < 3:
                mpb[i, h * 128 : (h + 1) * 128, :] = m.astype(bf16)
            else:
                M0[h * 128 : (h + 1) * 128, :] = m
        if i < 3:
            x1(i).start()

    for i in range(3):
        n1(i).wait_recv()
    N2s[...] = N1s[...] + N1r[0] + N1r[1] + N1r[2]

    def n2(i):
        return remote(N2s, N2r.at[i], n2_send.at[i], n2_recv.at[i], yz_peers[i], band)

    for i in range(15):
        n2(i).start()

    acc = M0[...]
    for i in range(3):
        x1(i).wait_recv()
        acc = acc + X1[i].astype(f32)
    SF[...] = acc
    SB[...] = acc.astype(bf16)

    def x2(i):
        a, b = yz_off[i]
        row = (((zh + a) % N_ZH) * N_Y + (gy + b) % N_Y) * 16
        return remote(
            SB.at[pl.ds(pl.multiple_of(row, 16), 16)], X2.at[i], x2_send.at[i], x2_recv.at[i],
            yz_peers[i], band,
        )

    for i in range(15):
        x2(i).start()

    total = N2s[...]
    for i in range(15):
        n2(i).wait_recv()
        total = total + N2r[i]
    inverse = lax.rsqrt(total[0:1, :] + epsilon)
    out_ref[...] = (CO[...] * inverse)[0:OWNED].astype(bf16)

    m = SF[pl.ds(pl.multiple_of((zh * N_Y + gy) * 16, 16), 16), :]
    for i in range(15):
        x2(i).wait_recv()
        m = m + X2[i].astype(f32)
    margin_ref[...] = m * inverse

    @pl.when(has_below)
    def _():
        j_copy.wait_send()

    @pl.when(has_above)
    def _():
        u_copy.wait_send()

    def sent(k, carry):
        @pl.when(has_below)
        def _():
            down(k).wait_send()

        @pl.when(has_above)
        def _():
            up(k).wait_send()

        return carry

    lax.fori_loop(0, DEGREE, sent, 0)
    send_own(False)
    for dist in range(1, N_ZL):
        forward(dist, False)
    for i in range(3):
        n1(i).wait_send()
        x1(i).wait_send()
    for i in range(15):
        n2(i).wait_send()
        x2(i).wait_send()


def per_device(start_block, resident, cell_kernel, cell_scale, potential, cell_nodes, send_rows):
    vm = lambda shape, t: pltpu.VMEM(shape, t)
    dma = lambda n: pltpu.SemaphoreType.DMA((n,))
    vmem = pl.BlockSpec(memory_space=pltpu.VMEM)
    smem = pl.BlockSpec(memory_space=pltpu.SMEM)
    scratch = [
        vm((2, NRP, ORB), f32),
        vm((832, 256), bf16),
        vm((2, MR, 256), f32),
        vm((4, MR, ORB), f32),
        vm((NRP, ORB), f32),
        vm((NR, ORB), f32),
        vm((NRP, ORB), f32),
        vm((8, NRL), f32),
        vm((NR, OWNP), bf16),
        vm((OWNP, NRL), bf16),
        vm((NRL, KL), bf16),
        vm((OWNP, ORB), bf16),
        vm((KL, KL), bf16),
        vm((MR, KL), bf16),
        vm((MR, KR), bf16),
        vm((2, 112, KR), bf16),
        vm((4, MR, PLP), bf16),
        vm((4, PLP, PLP), f32),
        vm((4, MR, PLP), bf16),
        vm((PLP, PLP), bf16),
        vm((PLP, PLP), bf16),
        vm((2, PLP, PLP), bf16),
        vm((PLP, ORB), f32),
        vm((PLP, ORB), f32),
        vm((8, OWNP), f32),
        vm((8, KL), jnp.int32),
        vm((8, PLP), f32),
        vm((DEGREE, PLP, ORB), bf16),
        vm((DEGREE, PL, ORB), bf16),
        vm((DEGREE, PLP, ORB), bf16),
        vm((DEGREE, PLP, ORB), bf16),
        vm((8, PLP), f32),
        vm((8, PLP), f32),
        vm((16, PLP), f32),
        vm((16, PLP), f32),
        vm((8, OWNP, ORB), bf16),
        vm((NRL, 256), bf16),
        vm((OWNP, ORB), bf16),
        vm((OWNP, ORB), f32),
        vm((3, 256, ORB), bf16),
        vm((3, 256, ORB), bf16),
        vm((256, ORB), f32),
        vm((256, ORB), f32),
        vm((256, ORB), bf16),
        vm((15, 16, ORB), bf16),
        vm((8, ORB), f32),
        vm((3, 8, ORB), f32),
        vm((8, ORB), f32),
        vm((15, 8, ORB), f32),
        dma(8), dma(8), dma(8), dma(8), dma(2), dma(2), dma(20), dma(8),
        dma(3), dma(3), dma(15), dma(15), dma(3), dma(3), dma(15), dma(15),
    ]
    return pl.pallas_call(
        kernel,
        out_shape=(
            jax.ShapeDtypeStruct((OWNED, ORB), bf16),
            jax.ShapeDtypeStruct((16, ORB), f32),
        ),
        in_specs=[vmem, vmem, vmem, smem, vmem, vmem, smem, vmem],
        out_specs=(vmem, vmem),
        scratch_shapes=scratch,
        compiler_params=pltpu.CompilerParams(
            collective_id=0, has_side_effects=True, vmem_limit_bytes=56 * 1024 * 1024
        ),
        cost_estimate=pl.CostEstimate(
            flops=4_000_000_000, bytes_accessed=1_000_000, transcendentals=128
        ),
    )(
        start_block, resident, cell_kernel, cell_scale, potential.reshape(1, OWNED), cell_nodes,
        cell_nodes, send_rows.reshape(1, PLANE),
    )


def solution(mesh):
    return jax.shard_map(
        per_device,
        mesh=mesh,
        in_specs=(
            P("domain", "band"),
            P("domain", "band"),
            P(),
            P("domain"),
            P("domain"),
            P("domain", None),
            P("domain"),
        ),
        out_specs=(P("domain", "band"), P("domain", "band")),
        check_vma=False,
    )
```

time: 763 us -> 100 us (0.13)
  the two profiles are of different devices: /device:TPU:128 before, /device:TPU:6 now
where the time goes in v1:
time: 100 us
  Pallas kernels  97.3 us (97%)
  local copies, waits for them, and re-layouts  2.27 us (2%)
    pallas_call x1, Pallas kernels, per_device(): pl.pallas_call(kernel, out_shape=(jax.ShapeDtypeStruct((OWNED, ORB), bf16...  97.3 us
    unnamed x4, local copies, waits for them, and re-layouts  2.27 us

profile of v1, /device:TPU:6, one launch (start us, length us, event | category | flops | bytes accessed | tf_op | source)
XLA Modules:
  0.0 100.2 jit_solution(17938119934180111269)
XLA Ops:
  0.6 97.3 %shard_map.86 = (bf16[1014,128]{1,0:T(8,128)(2,1)}, f32[16,128]{1,0:T(8,128)}) custom-call(bf16[1014,128]{1,0:T(8,128)(2,1)} %start_ref.1, bf16[1014,128]{1,0:T(8,128)(2,1)} %res_ref.1, bf16[343,343]{1,0:T(8,128)(2,1)} %ck_ref.1, f32[4]{0:T(128)} %scale_ref.1, f32[1,1014]{1,0:T(1,128)} %bitcast.2, s32[4,343]{1,0:T(4,128)} %cns_ref.1, s32[4,343]{1,0:T(4,128)} %cns_ref.1, ...), custom_call_target="tpu_custom_call" | custom-call | flops 4000000000 | bytes 1000000 | tf_op jit(solution)/shard_map/pallas_call | solution.py:718
  97.9 0.0 copy-start
  97.9 1.7 %copy.11 = bf16[1014,128]{1,0:T(8,128)(2,1)} copy(bf16[1014,128]{1,0:T(8,128)(2,1)} %get-tuple-element.4) | data formatting | bytes 519168
  99.6 0.0 copy-done
  99.6 0.6 copy.12
Async XLA Ops:
  97.9 1.7 %copy-start = (f32[16,128]{1,0:T(8,128)S(1)}, f32[16,128]{1,0:T(8,128)}, u32[]{:S(2)}) copy-start(f32[16,128]{1,0:T(8,128)} %get-tuple-element.5) | copy-start | bytes 24580

commit v2 on v1

--- a/solution.py
+++ b/solution.py
@@ -88,7 +88,7 @@
     out_ref, margin_ref,
     V, R, O, OG, part, potc, place, prow, Pm, PT, Q, st, kpad, K1, Kp, T, KgP, KttP, KgD,
     ET, F, W2, top_col, jbot_col, pot8, cnp, srp,
-    Gs, cs, Gr, cr, Js, Jr, Us, Ur, RB, H2, LOW, CO, mpb, X1, M0, SF, SB, X2, N1s, N1r, N2s, N2r,
+    R2, KgB, M1T, CR, Ps, Qs, Gs, cs, Gr, cr, Js, Jr, Us, Ur, RB, H2, LOW, CO, mpb, X1, M0, SF, SB, X2, N1s, N1r, N2s, N2r,
     g_send, g_recv, c_send, c_recv, j_sem, u_sem, r_send, r_recv, x1_send, x1_recv, x2_send, x2_recv,
     n1_send, n1_recv, n2_send, n2_recv,
 ):
@@ -102,6 +102,8 @@
     sibling = zl * 2 + (1 - core)
     has_below = d > 0
     has_above = d < N_DOM - 1
+    lower = d == N_DOM // N_ZH - 1
+    upper = d == N_DOM // N_ZH
 
     Gr[...] = jnp.zeros_like(Gr)
     cr[...] = jnp.zeros_like(cr)
@@ -249,13 +251,6 @@
     RB[band, 1008:1024, :] = jnp.zeros((16, ORB), bf16)
     RB[band, 0:OWNED, :] = res_ref[...]
 
-    ones = lambda cond: jnp.where(cond, 1, 0)
-    count = (
-        ones(has_below) + ones(has_above) + ones(zl > 0) + ones(zl < N_ZL - 1)
-        + 1 + len(x_peers) + len(yz_peers)
-    )
-    pl.semaphore_wait(barrier, count)
-
     def remote(src, dst, ssem, rsem, dom, bnd):
         return pltpu.make_async_remote_copy(
             src_ref=src, dst_ref=dst, send_sem=ssem, recv_sem=rsem,
@@ -265,14 +260,6 @@
     j_copy = remote(Js, Jr, j_sem.at[0], j_sem.at[1], d - 1, band)
     u_copy = remote(Us, Ur, u_sem.at[0], u_sem.at[1], d + 1, band)
 
-    @pl.when(has_below)
-    def _():
-        j_copy.start()
-
-    @pl.when(has_above)
-    def _():
-        u_copy.start()
-
     def block(src, to, s):
         return remote(RB.at[src], RB.at[src], r_send.at[s], r_recv.at[src], d, to)
 
@@ -318,8 +305,6 @@
 
             c = block(src, sibling, 10 + 3 * dist)
             c.start() if start else c.wait_send()
-
-    send_own(True)
 
     st[1008:1024, :] = jnp.zeros((16, ORB), bf16)
     st[0:OWNED, :] = start_ref[...]
@@ -354,37 +339,77 @@
         t_hot = jnp.concatenate([hot(kt == -x) for x in range(7)], 0)
         T[cy] = mm_nt(mm(t_hot, kmat).astype(bf16), col_hot).astype(bf16)
 
-    def down(k):
+    def down(k, src):
         return remote(
-            Gs.at[k, pl.ds(0, PL)], Gr.at[k, pl.ds(0, PL)], g_send.at[k], g_recv.at[k], d - 1, band
+            src.at[k, pl.ds(0, PL)], Gr.at[k, pl.ds(0, PL)], g_send.at[k], g_recv.at[k], d - 1, band
         )
 
-    def up(k):
-        return remote(cs.at[k], cr.at[k, pl.ds(0, PL)], c_send.at[k], c_recv.at[k], d + 1, band)
+    def up(k, src):
+        return remote(
+            src.at[k, pl.ds(0, PL)], cr.at[k, pl.ds(0, PL)], c_send.at[k], c_recv.at[k], d + 1, band
+        )
+
+    def lowest_plane(v, out, k):
+        for X in range(NX):
+            lo = v[pl.ds(X * XS, 8, stride=8), :]
+            hi = v[pl.ds(X * XS + 64, 8, stride=8), :]
+            out[k, X * 16 : X * 16 + 16, :] = jnp.concatenate([lo, hi], 0).astype(bf16)
+
+    def top_sums(r, sc):
+        c0 = mm(T[0], r[0:KR, 0:128]) * sc[0] + mm(T[1], r[0:KR, 128:256]) * sc[2]
+        c1 = mm(T[0], r[384 : 384 + KR, 0:128]) * sc[1]
+        c1 = c1 + mm(T[1], r[384 : 384 + KR, 128:256]) * sc[3]
+        return ((0, 96, c0[0:96]), (96, 112, c0[96:112] + c1[0:16]), (112, 208, c1[16:112]))
+
+    def prepare_down(k, cur):
+        Gs[k, PL:PLP, :] = jnp.zeros((PLP - PL, ORB), bf16)
+        lowest_plane(V.at[cur], Gs, k)
+
+    def prepare_up(k):
+        cs[k, PL:PLP, :] = jnp.zeros((PLP - PL, ORB), bf16)
+        for lo, hi, value in top_sums(R, scale):
+            cs[k, lo:hi, :] = value.astype(bf16)
 
     def send_planes(k, cur):
-        Gs[k, PL:PLP, :] = jnp.zeros((PLP - PL, ORB), bf16)
-        for X in range(NX):
-            lo = V[cur, pl.ds(X * XS, 8, stride=8), :]
-            hi = V[cur, pl.ds(X * XS + 64, 8, stride=8), :]
-            Gs[k, X * 16 : X * 16 + 16, :] = jnp.concatenate([lo, hi], 0).astype(bf16)
-
-        @pl.when(has_below)
-        def _():
-            down(k).start()
-
-        c0 = mm(T[0], R[0:KR, 0:128]) * scale[0] + mm(T[1], R[0:KR, 128:256]) * scale[2]
-        c1 = mm(T[0], R[384 : 384 + KR, 0:128]) * scale[1]
-        c1 = c1 + mm(T[1], R[384 : 384 + KR, 128:256]) * scale[3]
-        cs[k, 0:96, :] = c0[0:96].astype(bf16)
-        cs[k, 96:112, :] = (c0[96:112] + c1[0:16]).astype(bf16)
-        cs[k, 112:208, :] = c1[16:112].astype(bf16)
-
-        @pl.when(has_above)
-        def _():
-            up(k).start()
-
-    send_planes(0, 0)
+        prepare_down(k, cur)
+
+        @pl.when(has_below & jnp.logical_not(upper))
+        def _():
+            down(k, Gs).start()
+
+        prepare_up(k)
+
+        @pl.when(has_above & jnp.logical_not(lower))
+        def _():
+            up(k, cs).start()
+
+    prepare_down(0, 0)
+    prepare_up(0)
+
+    ones = lambda cond: jnp.where(cond, 1, 0)
+    count = (
+        ones(has_below) + ones(has_above) + ones(zl > 0) + ones(zl < N_ZL - 1)
+        + 1 + len(x_peers) + len(yz_peers)
+    )
+    pl.semaphore_wait(barrier, count)
+
+    @pl.when(has_below)
+    def _():
+        down(0, Gs).start()
+
+    @pl.when(has_above)
+    def _():
+        up(0, cs).start()
+
+    @pl.when(has_below)
+    def _():
+        j_copy.start()
+
+    @pl.when(has_above)
+    def _():
+        u_copy.start()
+
+    send_own(True)
 
     pot8[...] = jnp.zeros_like(pot8)
     pot = pot_ref[...]
@@ -448,6 +473,16 @@
     w_hi = w.astype(bf16)
     w_lo = (w - w_hi.astype(f32)).astype(bf16)
     fm = F[...]
+    @pl.when(lower)
+    def _():
+        eye = hot(iota((PLP, PLP), 0) == iota((PLP, PLP), 1))
+        M1T[...] = mm_nt(eye, m1).astype(bf16)
+
+    @pl.when(upper)
+    def _():
+        for c in range(4):
+            KgB[c] = mm_nt(KgP[c], F[...]).astype(bf16)
+
     W2[0] = mm_nt(mm(fm, w_hi).astype(bf16), fm).astype(bf16)
     W2[1] = mm_nt(mm(fm, w_lo).astype(bf16), fm).astype(bf16)
 
@@ -486,56 +521,116 @@
         g = Gs[k]
         return (mm(W2[0], g) + mm(W2[1], g)) * a
 
+    def add_plane(v, e):
+        for X in range(NX):
+            lo = pl.ds(X * XS, 8, stride=8)
+            hi = pl.ds(X * XS + 64, 8, stride=8)
+            v[lo, :] = v[lo, :] + e[X * 16 : X * 16 + 8]
+            v[hi, :] = v[hi, :] + e[X * 16 + 8 : X * 16 + 16]
+
+    def to_operand(r, X, flat):
+        r[X * 64 : X * 64 + 64, 0:128] = flat[0:64].astype(bf16)
+        r[X * 64 : X * 64 + 64, 128:256] = jnp.concatenate([flat[48:104], zero8], 0).astype(bf16)
+
+    def ghost(X, am, sc):
+        return spread(
+            lambda cx, cy, x: OG[cx + 2 * cy, x * 56 : x * 56 + 56, :],
+            X,
+            lambda cx, cy: (am * sc[cx + 2 * cy])[None],
+        )
+
+    def ahead(k):
+        am = mask8 * pick(k - 1, [t[0] for t in TERMS])
+        sb = [Ur[8 + c : 9 + c, 0:128] for c in range(4)]
+        for c in range(4):
+            OG[c] = mm(KgB[c], Gs[k - 1])
+        for X in range(NX):
+            to_operand(R2, X, ghost(X, am, sb).reshape(104, ORB))
+        for lo, hi, value in top_sums(R2, sb):
+            CR[lo:hi, :] = value
+
     def finish(k, cur, plane, last):
         nxt = 1 - cur
         a = pick(k, [t[0] for t in TERMS])
         am = mask8 * a
 
-        @pl.when(has_below)
-        def _():
-            up(k).wait_recv()
-
-        e = plane + mm(F[...], cr[k]) * a
-        for X in range(NX):
-            lo = pl.ds(X * XS, 8, stride=8)
-            hi = pl.ds(X * XS + 64, 8, stride=8)
-            part[lo, :] = part[lo, :] + e[X * 16 : X * 16 + 8]
-            part[hi, :] = part[hi, :] + e[X * 16 + 8 : X * 16 + 16]
+        @pl.when(upper)
+        def _():
+            add_plane(part, plane)
+
+        @pl.when(jnp.logical_not(upper))
+        def _():
+            @pl.when(has_below)
+            def _():
+                up(k, cs).wait_recv()
+
+            add_plane(part, plane + mm(F[...], cr[k]) * a)
+
+        if not last:
+
+            @pl.when(lower)
+            def _():
+                for X in range(NX):
+                    to_operand(R2, X, part[X * XS : X * XS + 104, :])
+                for lo, hi, value in top_sums(R2, scale):
+                    Ps[k + 1, lo:hi, :] = value.astype(bf16)
+                up(k + 1, Ps).start()
 
         @pl.when(has_above)
         def _():
-            down(k).wait_recv()
+            down(k, Gs).wait_recv()
+
+        @pl.when(lower & (k >= 1))
+        def _():
+            before = pick(k - 1, [t[0] for t in TERMS])
+            Gr[k] = (Gr[k].astype(f32) + mm(M1T[...], cs[k - 1]) * before).astype(bf16)
 
         for c in range(4):
             OG[c] = mm(KgD[c], Gr[k])
+        for X in range(NX):
+            rows = slice(X * XS, X * XS + 104)
+            new = part[rows, :].reshape(NX, 8, ORB) + ghost(X, am, scale)
+            flat = new.reshape(104, ORB)
+            V[nxt, rows, :] = flat
+            if not last:
+                to_operand(R, X, flat)
+
+        @pl.when(upper)
+        def _():
+            if not last:
+                lowest_plane(V.at[nxt], Qs, k + 1)
+                down(k + 1, Qs).start()
+            up(k, cs).wait_recv()
+
+            @pl.when(k >= 1)
+            def _():
+                cr[k, 0:PL, :] = (cr[k, 0:PL, :].astype(f32) + CR[...]).astype(bf16)
+
+            add_plane(V.at[nxt], mm(F[...], cr[k]) * a)
+            if not last:
+                for X in range(NX):
+                    to_operand(R, X, V[nxt, X * XS : X * XS + 104, :])
+
+        if not last:
+            return None
         sq = jnp.zeros((8, ORB), f32)
         for X in range(NX):
-            rows = slice(X * XS, X * XS + 104)
-            s = spread(
-                lambda cx, cy, x: OG[cx + 2 * cy, x * 56 : x * 56 + 56, :],
-                X,
-                lambda cx, cy: (am * scale[cx + 2 * cy])[None],
-            )
-            new = part[rows, :].reshape(NX, 8, ORB) + s
-            flat = new.reshape(104, ORB)
-            if last:
-                sq = sq + jnp.sum(new * new, 0)
-                padded = jnp.concatenate([flat, zero8], 0)
-                top = padded.astype(bf16)
-                H2[X * XS : (X + 1) * XS, 0:128] = top
-                H2[X * XS : (X + 1) * XS, 128:256] = (padded - top.astype(f32)).astype(bf16)
-            else:
-                V[nxt, rows, :] = flat
-                R[X * 64 : X * 64 + 64, 0:128] = flat[0:64].astype(bf16)
-                R[X * 64 : X * 64 + 64, 128:256] = jnp.concatenate(
-                    [flat[48:104], zero8], 0
-                ).astype(bf16)
+            padded = V[nxt, X * XS : (X + 1) * XS, :]
+            cube = padded.reshape(NX + 1, 8, ORB)
+            sq = sq + jnp.sum(cube * cube, 0)
+            top = padded.astype(bf16)
+            H2[X * XS : (X + 1) * XS, 0:128] = top
+            H2[X * XS : (X + 1) * XS, 128:256] = (padded - top.astype(f32)).astype(bf16)
         return sq
 
     def step(k, carry):
         cur = lax.rem(k, 2)
         plane = bulk(k, cur)
 
+        @pl.when(upper & (k >= 1))
+        def _():
+            ahead(k)
+
         @pl.when(k == 3)
         def _():
             forward(1, True)
@@ -551,6 +646,11 @@
     lax.fori_loop(0, DEGREE - 1, step, 0)
     final = DEGREE - 1
     plane = bulk(final, final % 2)
+
+    @pl.when(upper)
+    def _():
+        ahead(final)
+
     forward(3, True)
     H2[NR:NRL, :] = jnp.zeros((NRL - NR, 256), bf16)
     sq = finish(final, final % 2, plane, True)
@@ -637,11 +737,11 @@
     def sent(k, carry):
         @pl.when(has_below)
         def _():
-            down(k).wait_send()
+            down(k, Gs).wait_send()
 
         @pl.when(has_above)
         def _():
-            up(k).wait_send()
+            up(k, cs).wait_send()
 
         return carry
 
@@ -690,8 +790,14 @@
         vm((8, OWNP), f32),
         vm((8, KL), jnp.int32),
         vm((8, PLP), f32),
+        vm((832, 256), bf16),
+        vm((4, MR, PLP), bf16),
+        vm((PLP, PLP), bf16),
+        vm((PL, ORB), f32),
+        vm((DEGREE, PL, ORB), bf16),
+        vm((DEGREE, PL, ORB), bf16),
         vm((DEGREE, PLP, ORB), bf16),
-        vm((DEGREE, PL, ORB), bf16),
+        vm((DEGREE, PLP, ORB), bf16),
         vm((DEGREE, PLP, ORB), bf16),
         vm((DEGREE, PLP, ORB), bf16),
         vm((8, PLP), f32),

time: 100 us -> 82.9 us (0.83); the launches traced: 100 us -> 81.9 us
  Pallas kernels: 97.3 us -> 79 us
    pallas_call x1, Pallas kernels: 97.3 us -> 79 us  [per_device(): pl.pallas_call(kernel, out_shape=(jax.ShapeDtypeStruct((OWNED, ORB), bf16...]
where the time goes in v2:
time: 82.9 us; the launch traced here: 81.9 us
  Pallas kernels  79 us (95%)
  local copies, waits for them, and re-layouts  2.27 us (3%)
    pallas_call x1, Pallas kernels, per_device(): pl.pallas_call(kernel, out_shape=(jax.ShapeDtypeStruct((OWNED, ORB), bf16...  79 us
    unnamed x4, local copies, waits for them, and re-layouts  2.27 us

profile of v2, /device:TPU:6, one launch (start us, length us, event | category | flops | bytes accessed | tf_op | source)
XLA Modules:
  0.0 81.9 jit_solution(2186286796132129980)
XLA Ops:
  0.6 79.0 %shard_map.86 = (bf16[1014,128]{1,0:T(8,128)(2,1)}, f32[16,128]{1,0:T(8,128)}) custom-call(bf16[1014,128]{1,0:T(8,128)(2,1)} %start_ref.1, bf16[1014,128]{1,0:T(8,128)(2,1)} %res_ref.1, bf16[343,343]{1,0:T(8,128)(2,1)} %ck_ref.1, f32[4]{0:T(128)} %scale_ref.1, f32[1,1014]{1,0:T(1,128)} %bitcast.2, s32[4,343]{1,0:T(4,128)} %cns_ref.1, s32[4,343]{1,0:T(4,128)} %cns_ref.1, ...), custom_call_target="tpu_custom_call" | custom-call | flops 4000000000 | bytes 1000000 | tf_op jit(solution)/shard_map/pallas_call | solution.py:824
  79.6 0.0 copy-start
  79.7 1.7 %copy.11 = bf16[1014,128]{1,0:T(8,128)(2,1)} copy(bf16[1014,128]{1,0:T(8,128)(2,1)} %get-tuple-element.4) | data formatting | bytes 519168
  81.3 0.0 copy-done
  81.3 0.6 copy.12
Async XLA Ops:
  79.6 1.7 %copy-start = (f32[16,128]{1,0:T(8,128)S(1)}, f32[16,128]{1,0:T(8,128)}, u32[]{:S(2)}) copy-start(f32[16,128]{1,0:T(8,128)} %get-tuple-element.5) | copy-start | bytes 24580

commit v3 on v2

--- a/solution.py
+++ b/solution.py
@@ -84,13 +84,14 @@
 
 
 def kernel(
-    start_ref, res_ref, ck_ref, scale_ref, pot_ref, cn_ref, cns_ref, sr_ref,
+    start_hbm, res_hbm, ck_hbm, scale_hbm, pot_hbm, cn_hbm, sr_hbm,
     out_ref, margin_ref,
+    start_ref, res_ref, ck_ref, scale_ref, pot_ref, cn_ref, cns_ref, sr_ref, OUT,
     V, R, O, OG, part, potc, place, prow, Pm, PT, Q, st, kpad, K1, Kp, T, KgP, KttP, KgD,
     ET, F, W2, top_col, jbot_col, pot8, cnp, srp,
-    R2, KgB, M1T, CR, Ps, Qs, Gs, cs, Gr, cr, Js, Jr, Us, Ur, RB, H2, LOW, CO, mpb, X1, M0, SF, SB, X2, N1s, N1r, N2s, N2r,
+    RBT, R2, KgB, M1T, D2, CR, CR2, Ps, Qs, Gs, cs, Gr, cr, Js, Jr, Us, Ur, RB, H2, LOW, CO, mpb, X1, M0, SF, SB, X2, N1s, N1r, N2s, N2r,
     g_send, g_recv, c_send, c_recv, j_sem, u_sem, r_send, r_recv, x1_send, x1_recv, x2_send, x2_recv,
-    n1_send, n1_recv, n2_send, n2_recv,
+    n1_send, n1_recv, n2_send, n2_recv, in_sem, out_sem,
 ):
     d = lax.axis_index("domain")
     band = lax.axis_index("band")
@@ -102,8 +103,21 @@
     sibling = zl * 2 + (1 - core)
     has_below = d > 0
     has_above = d < N_DOM - 1
-    lower = d == N_DOM // N_ZH - 1
-    upper = d == N_DOM // N_ZH
+    mid = N_DOM // N_ZH
+    end_y = has_above & (d % N_Y == N_Y - 1)
+    first_y = has_below & (d % N_Y == 0)
+    up_early = end_y | (d == mid - 2)
+    up_mend = first_y | (d == mid - 1)
+    down_early = first_y | (d == mid + 1)
+    down_mend = end_y | (d == mid)
+
+    given = [
+        (cn_hbm, cns_ref), (cn_hbm, cn_ref), (scale_hbm, scale_ref), (sr_hbm, sr_ref),
+        (start_hbm, start_ref), (ck_hbm, ck_ref), (res_hbm, res_ref), (pot_hbm, pot_ref),
+    ]
+    given = [pltpu.make_async_copy(a, b, in_sem.at[i]) for i, (a, b) in enumerate(given)]
+    for c in given:
+        c.start()
 
     Gr[...] = jnp.zeros_like(Gr)
     cr[...] = jnp.zeros_like(cr)
@@ -123,6 +137,9 @@
         (((zh + a) % N_ZH) * N_X + gx) * N_Y + (gy + b) % N_Y for a, b in yz_off
     ]
 
+    for p in yz_peers[::-1] + x_peers:
+        greet(p, band)
+
     @pl.when(has_below)
     def _():
         greet(d - 1, band)
@@ -140,9 +157,9 @@
         greet(d, band + 2)
 
     greet(d, sibling)
-    for p in x_peers + yz_peers:
-        greet(p, band)
-
+
+    for c in given[0:3]:
+        c.wait()
     corner = [cns_ref[c, 0] for c in range(4)]
     right_x = [cns_ref[c, EDGE - 1] for c in range(4)]
     right_y = [cns_ref[c, EDGE * (EDGE - 1)] for c in range(4)]
@@ -197,6 +214,7 @@
             Pm[X * XS : (X + 1) * XS, t * 128 : (t + 1) * 128] = hot(own == lane + 128.0 * t)
     place[NR:NRP, :] = jnp.full((NRP - NR, 128), -1.0, f32)
 
+    given[3].wait()
     srp[...] = jnp.full(srp.shape, -5.0, f32)
     srp[0:1, 0:PLANE] = sr_ref[...].astype(f32)
     top_col[...] = jnp.full(top_col.shape, -1.0, f32)
@@ -213,10 +231,10 @@
                 b0 == srp[0:1, t * 128 : (t + 1) * 128]
             )
         t0 = jnp.concatenate(
-            [place[pl.ds(X * XS + 6, 8, stride=8), :], place[pl.ds(X * XS + 70, 8, stride=8), :]],
+            [place[pl.ds(X * XS + 6, 8, stride=8), :], place[pl.ds(X * XS + 54, 8, stride=8), :]],
             0,
         )
-        top_col[X * 16 : X * 16 + 16, :] = jnp.where(yrow < NX, t0 - float(OWNED), -1.0)
+        top_col[X * 16 : X * 16 + 16, :] = jnp.where((yrow & 7) < EDGE, t0 - float(OWNED), -1.0)
     jm = iota((PLP, 128), 0).astype(f32).astype(bf16)
     p_row = iota((PLP, 128), 0)
     jb = mm(ET[...], jm)
@@ -230,24 +248,26 @@
     pln = iota((PLP, KL), 1)
     pX = pr >> 4
     pY = pr & 15
-    p_in = (pX < NX) & (pY < NX)
+    ty = pr & 7
+    tcy = (pr >> 3) & 1
+    t_in = (pX < NX) & (ty < EDGE)
     ox = jnp.where(pX > 6, pX - 6, pX)
-    oy = jnp.where(pY > 6, pY - 6, pY)
-    q_top = hot(p_in & (294 + oy * 7 + ox == pln))
+    q_top = hot(t_in & (294 + ty * 7 + ox == pln))
     at = mm_nt(cn8, q_top)
     lX = p_lane >> 4
-    lY = p_lane & 15
-    l_cell = jnp.where(lX > 6, 1, 0) + jnp.where(lY > 6, 2, 0)
+    l_cell = jnp.where(lX > 6, 1, 0) + ((p_lane >> 3) & 1) * 2
+    t_ok = ((p_lane & 7) < EDGE) & (p_lane < PL)
     r8 = iota((8, PLP), 0)
     at = jnp.where((r8 & 3) == l_cell, at, 0.0) * jnp.where(r8 < 4, 32.0, 1.0)
     top_line = jnp.sum(at, 0, keepdims=True) - float(OWNED)
-    Us[0:8, :] = jnp.where(p_ok, jnp.broadcast_to(top_line, (8, PLP)), -1.0)
+    Us[0:8, :] = jnp.where(t_ok, jnp.broadcast_to(top_line, (8, PLP)), -1.0)
     srow = iota((8, PLP), 0)
     stile = jnp.zeros((8, PLP), f32)
     for c in range(4):
         stile = jnp.where(srow == c, scale[c], stile)
     Us[8:16, :] = stile
 
+    given[6].wait()
     RB[band, 1008:1024, :] = jnp.zeros((16, ORB), bf16)
     RB[band, 0:OWNED, :] = res_ref[...]
 
@@ -260,6 +280,27 @@
     j_copy = remote(Js, Jr, j_sem.at[0], j_sem.at[1], d - 1, band)
     u_copy = remote(Us, Ur, u_sem.at[0], u_sem.at[1], d + 1, band)
 
+    def turn(dist):
+        if dist == 0:
+            block(sibling, sibling, 0).wait_recv()
+            RBT[band] = RB[band].T
+            RBT[sibling] = RB[sibling].T
+            return
+
+        def both(src):
+            other = src + 1 - 2 * core
+            block(other, sibling, 0).wait_recv()
+            RBT[src] = RB[src].T
+            RBT[other] = RB[other].T
+
+        @pl.when(zl >= dist)
+        def _():
+            both(band - 2 * dist)
+
+        @pl.when(zl + dist <= N_ZL - 1)
+        def _():
+            both(band + 2 * dist)
+
     def block(src, to, s):
         return remote(RB.at[src], RB.at[src], r_send.at[s], r_recv.at[src], d, to)
 
@@ -306,6 +347,7 @@
             c = block(src, sibling, 10 + 3 * dist)
             c.start() if start else c.wait_send()
 
+    given[4].wait()
     st[1008:1024, :] = jnp.zeros((16, ORB), bf16)
     st[0:OWNED, :] = start_ref[...]
     V[0, 0:NR, :] = mm(Pm[...], st[...])
@@ -317,6 +359,7 @@
         R[X * 64 : X * 64 + 64, 0:128] = V[0, X * XS : X * XS + 64, :].astype(bf16)
         R[X * 64 : X * 64 + 64, 128:256] = V[0, X * XS + 48 : X * XS + 112, :].astype(bf16)
 
+    given[5].wait()
     kpad[...] = jnp.zeros_like(kpad)
     kpad[0:343, 0:343] = ck_ref[...]
     kmat = kpad[...]
@@ -331,13 +374,15 @@
     col_hot = jnp.concatenate([hot(k64 == -x) for x in range(7)], 0)
     K1[...] = mm(row_hot, kmat).astype(bf16)
     Kp[...] = mm_nt(K1[...], col_hot).astype(bf16)
-    r16 = iota((16, KL), 0)
-    l16 = iota((16, KL), 1)
-    for cy in range(2):
-        y = r16 - 6 * cy
-        kt = jnp.where((y >= 0) & (y < 7), 294 + y * 7, -1000) - l16
-        t_hot = jnp.concatenate([hot(kt == -x) for x in range(7)], 0)
-        T[cy] = mm_nt(mm(t_hot, kmat).astype(bf16), col_hot).astype(bf16)
+    r8k = iota((8, KL), 0)
+    l8k = iota((8, KL), 1)
+    kt = jnp.where(r8k < EDGE, 294 + r8k * 7, -1000) - l8k
+    kb = jnp.where(r8k < EDGE, r8k * 7, -1000) - l8k
+    none8 = jnp.zeros((8, KL), f32)
+    t_hot = jnp.concatenate([jnp.where(kt == -x, 1.0, 0.0) for x in range(7)] + [none8], 0).astype(bf16)
+    b_hot = jnp.concatenate([jnp.where(kb == -x, 1.0, 0.0) for x in range(7)] + [none8], 0).astype(bf16)
+    top_k = mm(t_hot, kmat).astype(bf16)
+    T[...] = mm_nt(top_k, col_hot)[0:56].astype(bf16)
 
     def down(k, src):
         return remote(
@@ -349,17 +394,30 @@
             src.at[k, pl.ds(0, PL)], cr.at[k, pl.ds(0, PL)], c_send.at[k], c_recv.at[k], d + 1, band
         )
 
-    def lowest_plane(v, out, k):
+    def lowest_plane(v, out, k, more=None):
         for X in range(NX):
             lo = v[pl.ds(X * XS, 8, stride=8), :]
             hi = v[pl.ds(X * XS + 64, 8, stride=8), :]
-            out[k, X * 16 : X * 16 + 16, :] = jnp.concatenate([lo, hi], 0).astype(bf16)
+            both = jnp.concatenate([lo, hi], 0)
+            if more is not None:
+                both = both + more[X * 16 : X * 16 + 16]
+            out[k, X * 16 : X * 16 + 16, :] = both.astype(bf16)
 
     def top_sums(r, sc):
-        c0 = mm(T[0], r[0:KR, 0:128]) * sc[0] + mm(T[1], r[0:KR, 128:256]) * sc[2]
-        c1 = mm(T[0], r[384 : 384 + KR, 0:128]) * sc[1]
-        c1 = c1 + mm(T[1], r[384 : 384 + KR, 128:256]) * sc[3]
-        return ((0, 96, c0[0:96]), (96, 112, c0[96:112] + c1[0:16]), (112, 208, c1[16:112]))
+        parts = [mm(T[...], r[384 * cx : 384 * cx + KR, :]) for cx in range(2)]
+        out = []
+        for X in range(NX):
+            tiles = []
+            for cy in range(2):
+                t = None
+                for cx in range(2):
+                    x = X - 6 * cx
+                    if 0 <= x < 7:
+                        p = parts[cx][x * 8 : x * 8 + 8, cy * 128 : (cy + 1) * 128] * sc[cx + 2 * cy]
+                        t = p if t is None else t + p
+                tiles.append(t)
+            out.append((X * 16, X * 16 + 16, jnp.concatenate(tiles, 0)))
+        return out
 
     def prepare_down(k, cur):
         Gs[k, PL:PLP, :] = jnp.zeros((PLP - PL, ORB), bf16)
@@ -370,16 +428,22 @@
         for lo, hi, value in top_sums(R, scale):
             cs[k, lo:hi, :] = value.astype(bf16)
 
+    def to_operand(r, X, flat):
+        r[X * 64 : X * 64 + 64, 0:128] = flat[0:64].astype(bf16)
+        r[X * 64 : X * 64 + 64, 128:256] = jnp.concatenate([flat[48:104], zero8], 0).astype(bf16)
+
     def send_planes(k, cur):
         prepare_down(k, cur)
 
-        @pl.when(has_below & jnp.logical_not(upper))
+        @pl.when(has_below & jnp.logical_not(down_early))
         def _():
             down(k, Gs).start()
 
+        for X in range(NX):
+            to_operand(R, X, V[cur, X * XS : X * XS + 104, :])
         prepare_up(k)
 
-        @pl.when(has_above & jnp.logical_not(lower))
+        @pl.when(has_above & jnp.logical_not(up_early))
         def _():
             up(k, cs).start()
 
@@ -411,6 +475,7 @@
 
     send_own(True)
 
+    given[7].wait()
     pot8[...] = jnp.zeros_like(pot8)
     pot = pot_ref[...]
     p_hi = pot.astype(bf16)
@@ -423,14 +488,25 @@
     pcol = mm_nt(Pm[...], pot8[...].astype(bf16)).astype(bf16)
     potc[...] = mm(pcol, jnp.ones((8, 128), bf16)) - CENTRE
 
+    q_l = iota((PLP, 64), 1)
+    q_p = iota((PLP, 64), 0)
+    q_in = ((q_l & 7) < EDGE) & (q_l < 56)
+
+    def in_top(c):
+        cx, cy = c % 2, c // 2
+        y_ok = (((q_p >> 3) & 1) == cy) & ((q_p & 7) == (q_l & 7))
+        return hot(((q_p >> 4) - 6 * cx == (q_l >> 3)) & y_ok & q_in)
+
+    def in_bottom(c):
+        cx, cy = c % 2, c // 2
+        return hot(((q_p >> 4) - 6 * cx == (q_l >> 3)) & ((q_p & 15) - 6 * cy == (q_l & 7)) & q_in)
+
+    k_tt = mm_nt(top_k, t_hot).astype(bf16)
+    k_g = mm_nt(K1[...], t_hot).astype(bf16)
     for c in range(4):
-        cx, cy = c % 2, c // 2
-        x = pX - 6 * cx
-        y = pY - 6 * cy
-        inside = (x >= 0) & (x < 7) & (y >= 0) & (y < 7)
-        c_top = hot(inside & (294 + y * 7 + x == pln))
-        KgP[c] = mm_nt(K1[...], c_top).astype(bf16)
-        KttP[c] = mm_nt(mm(c_top, kmat).astype(bf16), c_top)
+        e_top = in_top(c)
+        KgP[c] = mm_nt(k_g, e_top).astype(bf16)
+        KttP[c] = mm_nt(mm(e_top, k_tt).astype(bf16), e_top)
 
     lin = iota((8, NRL), 1)
     lin_x = jnp.floor((lin.astype(f32) + 0.5) * (1.0 / XS)).astype(jnp.int32)
@@ -451,40 +527,6 @@
         PT[pl.ds(pl.multiple_of(i * 16, 16), 16), :] = hot(prow[0:1, :] == n16 + base)
         return carry
 
-    lax.fori_loop(0, OWNP // 16, fill, 0)
-
-    @pl.when(has_above)
-    def _():
-        j_copy.wait_recv()
-
-    @pl.when(has_below)
-    def _():
-        u_copy.wait_recv()
-
-    tc = top_col[...]
-    jc = jbot_col[...]
-    m1 = jnp.concatenate([hot(tc == Jr[0:1, t * 128 : (t + 1) * 128]) for t in range(2)], 1)
-    F[...] = jnp.concatenate([hot(jc == Ur[0:1, t * 128 : (t + 1) * 128]) for t in range(2)], 1)
-    for c in range(4):
-        KgD[c] = mm(KgP[c], m1).astype(bf16)
-    w = jnp.zeros((PLP, PLP), f32)
-    for c in range(4):
-        w = w + KttP[c] * Ur[8 + c : 9 + c, :]
-    w_hi = w.astype(bf16)
-    w_lo = (w - w_hi.astype(f32)).astype(bf16)
-    fm = F[...]
-    @pl.when(lower)
-    def _():
-        eye = hot(iota((PLP, PLP), 0) == iota((PLP, PLP), 1))
-        M1T[...] = mm_nt(eye, m1).astype(bf16)
-
-    @pl.when(upper)
-    def _():
-        for c in range(4):
-            KgB[c] = mm_nt(KgP[c], F[...]).astype(bf16)
-
-    W2[0] = mm_nt(mm(fm, w_hi).astype(bf16), fm).astype(bf16)
-    W2[1] = mm_nt(mm(fm, w_lo).astype(bf16), fm).astype(bf16)
 
     mask8 = jnp.where(iota((8, ORB), 0) < EDGE - 1, 1.0, 0.0)
 
@@ -518,8 +560,67 @@
             pc = potc[rows, :].reshape(NX, 8, ORB)
             new = (s + pc * v) * am[None] - b * u
             part[rows, :] = new.reshape(104, ORB)
-        g = Gs[k]
-        return (mm(W2[0], g) + mm(W2[1], g)) * a
+
+    bulk(0, 0)
+
+    @pl.when(has_above)
+    def _():
+        j_copy.wait_recv()
+
+    @pl.when(has_below)
+    def _():
+        u_copy.wait_recv()
+
+    tc = top_col[...]
+    jc = jbot_col[...]
+    m1 = jnp.concatenate([hot(tc == Jr[0:1, t * 128 : (t + 1) * 128]) for t in range(2)], 1)
+    F[...] = jnp.concatenate([hot(jc == Ur[0:1, t * 128 : (t + 1) * 128]) for t in range(2)], 1)
+    for c in range(4):
+        KgD[c] = mm(KgP[c], m1).astype(bf16)
+    w = jnp.zeros((PLP, PLP), f32)
+    for c in range(4):
+        w = w + KttP[c] * Ur[8 + c : 9 + c, :]
+    w_hi = w.astype(bf16)
+    w_lo = (w - w_hi.astype(f32)).astype(bf16)
+    fm = F[...]
+    @pl.when(down_mend)
+    def _():
+        eye = hot(iota((PLP, PLP), 0) == iota((PLP, PLP), 1))
+        M1T[...] = mm_nt(eye, m1).astype(bf16)
+
+    @pl.when(up_mend)
+    def _():
+        for c in range(4):
+            KgB[c] = mm_nt(KgP[c], F[...]).astype(bf16)
+
+    w = mm_nt(mm(fm, w_hi).astype(bf16), fm) + mm_nt(mm(fm, w_lo).astype(bf16), fm)
+    w_hi = w.astype(bf16)
+    W2[0] = w_hi
+    W2[1] = (w - w_hi.astype(f32)).astype(bf16)
+
+    def plane_to_plane(rows_top, onward):
+        total = jnp.zeros((PLP, PLP), f32)
+        if rows_top:
+            block_k = mm_nt(top_k, b_hot).astype(bf16)
+        else:
+            block_k = mm_nt(mm(b_hot, kmat).astype(bf16), t_hot).astype(bf16)
+        for c in range(4):
+            one, two = (in_top(c), in_bottom(c)) if rows_top else (in_bottom(c), in_top(c))
+            total = total + mm_nt(mm(one, block_k).astype(bf16), two) * scale[c]
+        hi = total.astype(bf16)
+        lo = (total - hi.astype(f32)).astype(bf16)
+        total = mm(hi, onward) + mm(lo, onward)
+        hi = total.astype(bf16)
+        D2[0] = hi
+        D2[1] = (total - hi.astype(f32)).astype(bf16)
+
+    @pl.when(up_early)
+    def _():
+        plane_to_plane(True, F[...])
+
+    @pl.when(down_early)
+    def _():
+        plane_to_plane(False, m1)
 
     def add_plane(v, e):
         for X in range(NX):
@@ -527,10 +628,6 @@
             hi = pl.ds(X * XS + 64, 8, stride=8)
             v[lo, :] = v[lo, :] + e[X * 16 : X * 16 + 8]
             v[hi, :] = v[hi, :] + e[X * 16 + 8 : X * 16 + 16]
-
-    def to_operand(r, X, flat):
-        r[X * 64 : X * 64 + 64, 0:128] = flat[0:64].astype(bf16)
-        r[X * 64 : X * 64 + 64, 128:256] = jnp.concatenate([flat[48:104], zero8], 0).astype(bf16)
 
     def ghost(X, am, sc):
         return spread(
@@ -547,70 +644,86 @@
         for X in range(NX):
             to_operand(R2, X, ghost(X, am, sb).reshape(104, ORB))
         for lo, hi, value in top_sums(R2, sb):
-            CR[lo:hi, :] = value
-
-    def finish(k, cur, plane, last):
+            CR[lax.rem(k, 2), lo:hi, :] = value
+
+    def mend_sums(k):
+        cr[k, 0:PL, :] = (cr[k, 0:PL, :].astype(f32) + CR[lax.rem(k, 2)]).astype(bf16)
+
+    def mend_plane(k):
+        before = pick(k - 1, [t[0] for t in TERMS])
+        Gr[k] = (Gr[k].astype(f32) + mm(M1T[...], cs[k - 1]) * before).astype(bf16)
+
+    def early(k, last):
+        a = pick(k, [t[0] for t in TERMS])
+        g = Gs[k]
+        add_plane(part, (mm(W2[0], g) + mm(W2[1], g)) * a)
+        if last:
+            return
+
+        @pl.when(up_early)
+        def _():
+            for X in range(NX):
+                to_operand(R2, X, part[X * XS : X * XS + 104, :])
+            for lo, hi, value in top_sums(R2, scale):
+                CR2[lo:hi, :] = value
+
+            @pl.when(has_below)
+            def _():
+                up(k, cs).wait_recv()
+
+            @pl.when(up_mend & (k >= 1))
+            def _():
+                mend_sums(k)
+
+            more = (mm(D2[0], cr[k]) + mm(D2[1], cr[k])) * a
+            Ps[k + 1] = (CR2[...] + more[0:PL]).astype(bf16)
+            up(k + 1, Ps).start()
+
+        @pl.when(down_early)
+        def _():
+            @pl.when(has_above)
+            def _():
+                down(k, Gs).wait_recv()
+
+            @pl.when(down_mend & (k >= 1))
+            def _():
+                mend_plane(k)
+
+            more = (mm(D2[0], Gr[k]) + mm(D2[1], Gr[k])) * a
+            lowest_plane(part, Qs, k + 1, more)
+            down(k + 1, Qs).start()
+
+    def finish(k, cur, last):
         nxt = 1 - cur
         a = pick(k, [t[0] for t in TERMS])
         am = mask8 * a
-
-        @pl.when(upper)
-        def _():
-            add_plane(part, plane)
-
-        @pl.when(jnp.logical_not(upper))
-        def _():
-            @pl.when(has_below)
-            def _():
-                up(k, cs).wait_recv()
-
-            add_plane(part, plane + mm(F[...], cr[k]) * a)
-
-        if not last:
-
-            @pl.when(lower)
-            def _():
-                for X in range(NX):
-                    to_operand(R2, X, part[X * XS : X * XS + 104, :])
-                for lo, hi, value in top_sums(R2, scale):
-                    Ps[k + 1, lo:hi, :] = value.astype(bf16)
-                up(k + 1, Ps).start()
-
-        @pl.when(has_above)
+        rest_down = has_above if last else has_above & jnp.logical_not(down_early)
+        rest_up = has_below if last else has_below & jnp.logical_not(up_early)
+
+        @pl.when(rest_down)
         def _():
             down(k, Gs).wait_recv()
 
-        @pl.when(lower & (k >= 1))
-        def _():
-            before = pick(k - 1, [t[0] for t in TERMS])
-            Gr[k] = (Gr[k].astype(f32) + mm(M1T[...], cs[k - 1]) * before).astype(bf16)
+        @pl.when(rest_down & down_mend & (k >= 1))
+        def _():
+            mend_plane(k)
 
         for c in range(4):
             OG[c] = mm(KgD[c], Gr[k])
         for X in range(NX):
             rows = slice(X * XS, X * XS + 104)
             new = part[rows, :].reshape(NX, 8, ORB) + ghost(X, am, scale)
-            flat = new.reshape(104, ORB)
-            V[nxt, rows, :] = flat
-            if not last:
-                to_operand(R, X, flat)
-
-        @pl.when(upper)
-        def _():
-            if not last:
-                lowest_plane(V.at[nxt], Qs, k + 1)
-                down(k + 1, Qs).start()
+            V[nxt, rows, :] = new.reshape(104, ORB)
+
+        @pl.when(rest_up)
+        def _():
             up(k, cs).wait_recv()
 
-            @pl.when(k >= 1)
-            def _():
-                cr[k, 0:PL, :] = (cr[k, 0:PL, :].astype(f32) + CR[...]).astype(bf16)
-
-            add_plane(V.at[nxt], mm(F[...], cr[k]) * a)
-            if not last:
-                for X in range(NX):
-                    to_operand(R, X, V[nxt, X * XS : X * XS + 104, :])
-
+        @pl.when(rest_up & up_mend & (k >= 1))
+        def _():
+            mend_sums(k)
+
+        add_plane(V.at[nxt], mm(F[...], cr[k]) * a)
         if not last:
             return None
         sq = jnp.zeros((8, ORB), f32)
@@ -625,35 +738,37 @@
 
     def step(k, carry):
         cur = lax.rem(k, 2)
-        plane = bulk(k, cur)
-
-        @pl.when(upper & (k >= 1))
-        def _():
-            ahead(k)
-
-        @pl.when(k == 3)
-        def _():
-            forward(1, True)
-
-        @pl.when(k == 5)
-        def _():
-            forward(2, True)
-
-        finish(k, cur, plane, False)
+        early(k, False)
+
+        @pl.when(up_mend)
+        def _():
+            ahead(k + 1)
+
+        for dist in range(1, N_ZL - 1):
+
+            @pl.when(k == 2 * dist + 1)
+            def _(dist=dist):
+                forward(dist, True)
+
+        for dist in range(2):
+
+            @pl.when(k == 4 * dist + 2)
+            def _(dist=dist):
+                turn(dist)
+
+        lax.fori_loop(k * 10, jnp.minimum(k * 10 + 10, OWNP // 16), fill, 0)
+        finish(k, cur, False)
         send_planes(k + 1, 1 - cur)
+        bulk(k + 1, 1 - cur)
         return carry
 
     lax.fori_loop(0, DEGREE - 1, step, 0)
     final = DEGREE - 1
-    plane = bulk(final, final % 2)
-
-    @pl.when(upper)
-    def _():
-        ahead(final)
-
+    early(final, True)
     forward(3, True)
+    turn(2)
     H2[NR:NRL, :] = jnp.zeros((NRL - NR, 256), bf16)
-    sq = finish(final, final % 2, plane, True)
+    sq = finish(final, final % 2, True)
 
     N1s[...] = jnp.broadcast_to(jnp.sum(sq, 0, keepdims=True), (8, ORB))
 
@@ -663,21 +778,18 @@
     for i in range(3):
         n1(i).start()
 
+    turn(3)
     un = mm(PT[...], H2[...])
     LOW[...] = un[:, 0:128].astype(bf16)
     CO[...] = un[:, 0:128] + un[:, 128:256]
 
-    for i in range(N_ZL):
-        src = i * 2 + (1 - core)
-        block(src, sibling, 0).wait_recv()
-
     def x1(i):
         return remote(mpb.at[i], X1.at[i], x1_send.at[i], x1_recv.at[i], x_peers[i], band)
 
     for i in range(4):
         tx = (gx + 1 + i) % N_X
         for h in range(N_ZH):
-            m = mm_tn(RB[h * N_X + tx], LOW[...])
+            m = mm(RBT[h * N_X + tx], LOW[...])
             if i < 3:
                 mpb[i, h * 128 : (h + 1) * 128, :] = m.astype(bf16)
             else:
@@ -718,13 +830,16 @@
         n2(i).wait_recv()
         total = total + N2r[i]
     inverse = lax.rsqrt(total[0:1, :] + epsilon)
-    out_ref[...] = (CO[...] * inverse)[0:OWNED].astype(bf16)
+    OUT[...] = (CO[...] * inverse)[0:OWNED].astype(bf16)
+    out_copy = pltpu.make_async_copy(OUT, out_ref, out_sem.at[0])
+    out_copy.start()
 
     m = SF[pl.ds(pl.multiple_of((zh * N_Y + gy) * 16, 16), 16), :]
     for i in range(15):
         x2(i).wait_recv()
         m = m + X2[i].astype(f32)
     margin_ref[...] = m * inverse
+    out_copy.wait()
 
     @pl.when(has_below)
     def _():
@@ -761,8 +876,16 @@
     vm = lambda shape, t: pltpu.VMEM(shape, t)
     dma = lambda n: pltpu.SemaphoreType.DMA((n,))
     vmem = pl.BlockSpec(memory_space=pltpu.VMEM)
-    smem = pl.BlockSpec(memory_space=pltpu.SMEM)
     scratch = [
+        vm((OWNED, ORB), bf16),
+        vm((OWNED, ORB), bf16),
+        vm((343, 343), bf16),
+        pltpu.SMEM((4,), f32),
+        vm((1, OWNED), f32),
+        vm((4, 343), jnp.int32),
+        pltpu.SMEM((4, 343), jnp.int32),
+        vm((1, PLANE), jnp.int32),
+        vm((OWNED, ORB), bf16),
         vm((2, NRP, ORB), f32),
         vm((832, 256), bf16),
         vm((2, MR, 256), f32),
@@ -778,7 +901,7 @@
         vm((KL, KL), bf16),
         vm((MR, KL), bf16),
         vm((MR, KR), bf16),
-        vm((2, 112, KR), bf16),
+        vm((56, KR), bf16),
         vm((4, MR, PLP), bf16),
         vm((4, PLP, PLP), f32),
         vm((4, MR, PLP), bf16),
@@ -790,9 +913,12 @@
         vm((8, OWNP), f32),
         vm((8, KL), jnp.int32),
         vm((8, PLP), f32),
+        vm((8, ORB, OWNP), bf16),
         vm((832, 256), bf16),
         vm((4, MR, PLP), bf16),
         vm((PLP, PLP), bf16),
+        vm((2, PLP, PLP), bf16),
+        vm((2, PL, ORB), f32),
         vm((PL, ORB), f32),
         vm((DEGREE, PL, ORB), bf16),
         vm((DEGREE, PL, ORB), bf16),
@@ -819,7 +945,7 @@
         vm((8, ORB), f32),
         vm((15, 8, ORB), f32),
         dma(8), dma(8), dma(8), dma(8), dma(2), dma(2), dma(20), dma(8),
-        dma(3), dma(3), dma(15), dma(15), dma(3), dma(3), dma(15), dma(15),
+        dma(3), dma(3), dma(15), dma(15), dma(3), dma(3), dma(15), dma(15), dma(8), dma(1),
     ]
     return pl.pallas_call(
         kernel,
@@ -827,8 +953,8 @@
             jax.ShapeDtypeStruct((OWNED, ORB), bf16),
             jax.ShapeDtypeStruct((16, ORB), f32),
         ),
-        in_specs=[vmem, vmem, vmem, smem, vmem, vmem, smem, vmem],
-        out_specs=(vmem, vmem),
+        in_specs=[pl.BlockSpec(memory_space=pl.ANY)] * 7,
+        out_specs=(pl.BlockSpec(memory_space=pl.ANY), vmem),
         scratch_shapes=scratch,
         compiler_params=pltpu.CompilerParams(
             collective_id=0, has_side_effects=True, vmem_limit_bytes=56 * 1024 * 1024
@@ -838,7 +964,7 @@
         ),
     )(
         start_block, resident, cell_kernel, cell_scale, potential.reshape(1, OWNED), cell_nodes,
-        cell_nodes, send_rows.reshape(1, PLANE),
+        send_rows.reshape(1, PLANE),
     )
 
 

time: 82.9 us -> 81.3 us (0.981)
  no operation moved by 1% of the time
where the time goes in v3:
time: 81.3 us; the launch traced here: 81.2 us
  Pallas kernels  78.2 us (96%)
  local copies, waits for them, and re-layouts  2.27 us (3%)
    pallas_call x1, Pallas kernels, per_device(): pl.pallas_call(kernel, out_shape=(jax.ShapeDtypeStruct((OWNED, ORB), bf16...  78.2 us
    unnamed x4, local copies, waits for them, and re-layouts  2.27 us

profile of v3, /device:TPU:6, one launch (start us, length us, event | category | flops | bytes accessed | tf_op | source)
XLA Modules:
  0.0 81.2 jit_solution(13129902759887660924)
XLA Ops:
  0.6 78.2 %shard_map.86 = (bf16[1014,128]{1,0:T(8,128)(2,1)}, f32[16,128]{1,0:T(8,128)}) custom-call(bf16[1014,128]{1,0:T(8,128)(2,1)} %start_hbm.1, bf16[1014,128]{1,0:T(8,128)(2,1)} %res_hbm.1, bf16[343,343]{1,0:T(8,128)(2,1)} %ck_hbm.1, f32[4]{0:T(128)} %scale_hbm.1, f32[1,1014]{1,0:T(1,128)} %bitcast.2, s32[4,343]{1,0:T(4,128)} %cn_hbm.1, s32[1,169]{1,0:T(1,128)} %bitcast.3), custom_call_target="tpu_custom_call" | custom-call | flops 4000000000 | bytes 1000000 | tf_op jit(solution)/shard_map/pallas_call | solution.py:950
  78.9 0.0 copy-start
  78.9 1.7 %copy.11 = bf16[1014,128]{1,0:T(8,128)(2,1)} copy(bf16[1014,128]{1,0:T(8,128)(2,1)} %get-tuple-element.4) | data formatting | bytes 519168
  80.6 0.0 copy-done
  80.6 0.6 copy.12
Async XLA Ops:
  78.9 1.7 %copy-start = (f32[16,128]{1,0:T(8,128)S(1)}, f32[16,128]{1,0:T(8,128)}, u32[]{:S(2)}) copy-start(f32[16,128]{1,0:T(8,128)} %get-tuple-element.5) | copy-start | bytes 24580

commit v4 on v3

--- a/solution.py
+++ b/solution.py
@@ -89,9 +89,9 @@
     start_ref, res_ref, ck_ref, scale_ref, pot_ref, cn_ref, cns_ref, sr_ref, OUT,
     V, R, O, OG, part, potc, place, prow, Pm, PT, Q, st, kpad, K1, Kp, T, KgP, KttP, KgD,
     ET, F, W2, top_col, jbot_col, pot8, cnp, srp,
-    RBT, R2, KgB, M1T, D2, CR, CR2, Ps, Qs, Gs, cs, Gr, cr, Js, Jr, Us, Ur, RB, H2, LOW, CO, mpb, X1, M0, SF, SB, X2, N1s, N1r, N2s, N2r,
+    RBT, R2, KgB, M1, WT, M1T, D2, CR, CR2, Ps, Qs, Gs, cs, Gr, cr, Js, Jr, Us, Ur, RB, H2, LOW, CO, mpb, X1, M0, SF, SB, X2, SZ, X3, N1s, N1r, N2s, N2r, N3s, N3r,
     g_send, g_recv, c_send, c_recv, j_sem, u_sem, r_send, r_recv, x1_send, x1_recv, x2_send, x2_recv,
-    n1_send, n1_recv, n2_send, n2_recv, in_sem, out_sem,
+    n1_send, n1_recv, n2_send, n2_recv, n3_sem, x3_sem, in_sem, out_sem,
 ):
     d = lax.axis_index("domain")
     band = lax.axis_index("band")
@@ -131,13 +131,9 @@
         pl.semaphore_signal(barrier, inc=1, device_id=(dom, bnd), device_id_type=MESH)
 
     x_peers = [(zh * N_X + (gx + i) % N_X) * N_Y + gy for i in range(1, N_X)]
-    x_from = x_peers
-    yz_off = [(a, b) for a in range(N_ZH) for b in range(N_Y) if (a, b) != (0, 0)]
-    yz_peers = [
-        (((zh + a) % N_ZH) * N_X + gx) * N_Y + (gy + b) % N_Y for a, b in yz_off
-    ]
-
-    for p in yz_peers[::-1] + x_peers:
+    y_peers = [(zh * N_X + gx) * N_Y + (gy + i) % N_Y for i in range(1, N_Y)]
+    z_peer = ((1 - zh) * N_X + gx) * N_Y + gy
+    for p in [z_peer] + y_peers + x_peers:
         greet(p, band)
 
     @pl.when(has_below)
@@ -453,25 +449,25 @@
     ones = lambda cond: jnp.where(cond, 1, 0)
     count = (
         ones(has_below) + ones(has_above) + ones(zl > 0) + ones(zl < N_ZL - 1)
-        + 1 + len(x_peers) + len(yz_peers)
+        + 2 + len(x_peers) + len(y_peers)
     )
     pl.semaphore_wait(barrier, count)
 
     @pl.when(has_below)
     def _():
+        j_copy.start()
+
+    @pl.when(has_above)
+    def _():
+        u_copy.start()
+
+    @pl.when(has_below)
+    def _():
         down(0, Gs).start()
 
     @pl.when(has_above)
     def _():
         up(0, cs).start()
-
-    @pl.when(has_below)
-    def _():
-        j_copy.start()
-
-    @pl.when(has_above)
-    def _():
-        u_copy.start()
 
     send_own(True)
 
@@ -563,40 +559,9 @@
 
     bulk(0, 0)
 
-    @pl.when(has_above)
-    def _():
-        j_copy.wait_recv()
-
-    @pl.when(has_below)
-    def _():
-        u_copy.wait_recv()
-
-    tc = top_col[...]
-    jc = jbot_col[...]
-    m1 = jnp.concatenate([hot(tc == Jr[0:1, t * 128 : (t + 1) * 128]) for t in range(2)], 1)
-    F[...] = jnp.concatenate([hot(jc == Ur[0:1, t * 128 : (t + 1) * 128]) for t in range(2)], 1)
-    for c in range(4):
-        KgD[c] = mm(KgP[c], m1).astype(bf16)
-    w = jnp.zeros((PLP, PLP), f32)
-    for c in range(4):
-        w = w + KttP[c] * Ur[8 + c : 9 + c, :]
-    w_hi = w.astype(bf16)
-    w_lo = (w - w_hi.astype(f32)).astype(bf16)
-    fm = F[...]
-    @pl.when(down_mend)
-    def _():
-        eye = hot(iota((PLP, PLP), 0) == iota((PLP, PLP), 1))
-        M1T[...] = mm_nt(eye, m1).astype(bf16)
-
-    @pl.when(up_mend)
-    def _():
-        for c in range(4):
-            KgB[c] = mm_nt(KgP[c], F[...]).astype(bf16)
-
-    w = mm_nt(mm(fm, w_hi).astype(bf16), fm) + mm_nt(mm(fm, w_lo).astype(bf16), fm)
-    w_hi = w.astype(bf16)
-    W2[0] = w_hi
-    W2[1] = (w - w_hi.astype(f32)).astype(bf16)
+    def halves(v):
+        hi = v.astype(bf16)
+        return hi, (v - hi.astype(f32)).astype(bf16)
 
     def plane_to_plane(rows_top, onward):
         total = jnp.zeros((PLP, PLP), f32)
@@ -614,14 +579,6 @@
         D2[0] = hi
         D2[1] = (total - hi.astype(f32)).astype(bf16)
 
-    @pl.when(up_early)
-    def _():
-        plane_to_plane(True, F[...])
-
-    @pl.when(down_early)
-    def _():
-        plane_to_plane(False, m1)
-
     def add_plane(v, e):
         for X in range(NX):
             lo = pl.ds(X * XS, 8, stride=8)
@@ -651,16 +608,23 @@
 
     def mend_plane(k):
         before = pick(k - 1, [t[0] for t in TERMS])
-        Gr[k] = (Gr[k].astype(f32) + mm(M1T[...], cs[k - 1]) * before).astype(bf16)
-
-    def early(k, last):
+
+        @pl.when((k != 1) | (d != mid - 1))
+        def _():
+            Gr[k] = (Gr[k].astype(f32) + mm(M1T[...], cs[k - 1]) * before).astype(bf16)
+
+        @pl.when((k == 1) & (d == mid - 1))
+        def _():
+            own = mm(M1[...], Gr[0]).astype(bf16)
+            sums = cs[0].astype(f32) + mm(WT[0], own) + mm(WT[1], own)
+            Gr[k] = (Gr[k].astype(f32) + mm(M1T[...], sums.astype(bf16)) * before).astype(bf16)
+
+    def early_up(k):
         a = pick(k, [t[0] for t in TERMS])
         g = Gs[k]
         add_plane(part, (mm(W2[0], g) + mm(W2[1], g)) * a)
-        if last:
-            return
-
-        @pl.when(up_early)
+
+        @pl.when(up_early & (k < DEGREE - 1))
         def _():
             for X in range(NX):
                 to_operand(R2, X, part[X * XS : X * XS + 104, :])
@@ -679,19 +643,20 @@
             Ps[k + 1] = (CR2[...] + more[0:PL]).astype(bf16)
             up(k + 1, Ps).start()
 
-        @pl.when(down_early)
-        def _():
-            @pl.when(has_above)
-            def _():
-                down(k, Gs).wait_recv()
-
-            @pl.when(down_mend & (k >= 1))
-            def _():
-                mend_plane(k)
-
-            more = (mm(D2[0], Gr[k]) + mm(D2[1], Gr[k])) * a
-            lowest_plane(part, Qs, k + 1, more)
-            down(k + 1, Qs).start()
+    def early_down(k):
+        a = pick(k, [t[0] for t in TERMS])
+
+        @pl.when(has_above)
+        def _():
+            down(k, Gs).wait_recv()
+
+        @pl.when(down_mend & (k >= 1))
+        def _():
+            mend_plane(k)
+
+        more = (mm(D2[0], Gr[k]) + mm(D2[1], Gr[k])) * a
+        lowest_plane(part, Qs, k + 1, more)
+        down(k + 1, Qs).start()
 
     def finish(k, cur, last):
         nxt = 1 - cur
@@ -736,10 +701,67 @@
             H2[X * XS : (X + 1) * XS, 128:256] = (padded - top.astype(f32)).astype(bf16)
         return sq
 
+    @pl.when(has_above)
+    def _():
+        j_copy.wait_recv()
+
+    tc = top_col[...]
+    M1[...] = jnp.concatenate([hot(tc == Jr[0:1, t * 128 : (t + 1) * 128]) for t in range(2)], 1)
+
+    @pl.when(down_early)
+    def _():
+        plane_to_plane(False, M1[...])
+
+    @pl.when(d == mid)
+    def _():
+        early_down(0)
+
+    @pl.when(has_below)
+    def _():
+        u_copy.wait_recv()
+
+    jc = jbot_col[...]
+    F[...] = jnp.concatenate([hot(jc == Ur[0:1, t * 128 : (t + 1) * 128]) for t in range(2)], 1)
+
+    @pl.when(up_early)
+    def _():
+        plane_to_plane(True, F[...])
+
+    w = jnp.zeros((PLP, PLP), f32)
+    for c in range(4):
+        w = w + KttP[c] * Ur[8 + c : 9 + c, :]
+    fm = F[...]
+    w_hi, w_lo = halves(w)
+    w = mm_nt(mm(fm, w_hi).astype(bf16), fm) + mm_nt(mm(fm, w_lo).astype(bf16), fm)
+    W2[0], W2[1] = halves(w)
+    early_up(0)
+
+    @pl.when(down_early & (d != mid))
+    def _():
+        early_down(0)
+
+    for c in range(4):
+        KgD[c] = mm(KgP[c], M1[...]).astype(bf16)
+
+    @pl.when(down_mend)
+    def _():
+        eye = hot(iota((PLP, PLP), 0) == iota((PLP, PLP), 1))
+        M1T[...] = mm_nt(eye, M1[...]).astype(bf16)
+
+    @pl.when(d == mid - 1)
+    def _():
+        total = KttP[0] * scale[0]
+        for c in range(1, 4):
+            total = total + KttP[c] * scale[c]
+        WT[0], WT[1] = halves(total)
+
+    @pl.when(up_mend)
+    def _():
+        for c in range(4):
+            KgB[c] = mm_nt(KgP[c], F[...]).astype(bf16)
+
     def step(k, carry):
         cur = lax.rem(k, 2)
-        early(k, False)
-
         @pl.when(up_mend)
         def _():
             ahead(k + 1)
@@ -760,13 +782,19 @@
         finish(k, cur, False)
         send_planes(k + 1, 1 - cur)
         bulk(k + 1, 1 - cur)
+        early_up(k + 1)
+
+        @pl.when(down_early & (k + 1 < DEGREE - 1))
+        def _():
+            early_down(k + 1)
+
         return carry
 
     lax.fori_loop(0, DEGREE - 1, step, 0)
     final = DEGREE - 1
-    early(final, True)
     forward(3, True)
     turn(2)
+    turn(3)
     H2[NR:NRL, :] = jnp.zeros((NRL - NR, 256), bf16)
     sq = finish(final, final % 2, True)
 
@@ -778,68 +806,83 @@
     for i in range(3):
         n1(i).start()
 
-    turn(3)
-    un = mm(PT[...], H2[...])
-    LOW[...] = un[:, 0:128].astype(bf16)
-    CO[...] = un[:, 0:128] + un[:, 128:256]
-
-    def x1(i):
-        return remote(mpb.at[i], X1.at[i], x1_send.at[i], x1_recv.at[i], x_peers[i], band)
-
-    for i in range(4):
+    CO[...] = mm(PT[...], H2[...])
+    LOW[...] = CO[:, 0:128].astype(bf16)
+
+    def x1(i, h):
+        j = i * N_ZH + h
+        return remote(mpb.at[j], X1.at[j], x1_send.at[j], x1_recv.at[j], x_peers[i], band)
+
+    for i in (1, 0, 2, 3):
         tx = (gx + 1 + i) % N_X
         for h in range(N_ZH):
             m = mm(RBT[h * N_X + tx], LOW[...])
             if i < 3:
-                mpb[i, h * 128 : (h + 1) * 128, :] = m.astype(bf16)
+                mpb[i * N_ZH + h] = m.astype(bf16)
+                x1(i, h).start()
             else:
-                M0[h * 128 : (h + 1) * 128, :] = m
-        if i < 3:
-            x1(i).start()
+                M0[h] = m
 
     for i in range(3):
         n1(i).wait_recv()
     N2s[...] = N1s[...] + N1r[0] + N1r[1] + N1r[2]
 
     def n2(i):
-        return remote(N2s, N2r.at[i], n2_send.at[i], n2_recv.at[i], yz_peers[i], band)
-
-    for i in range(15):
+        return remote(N2s, N2r.at[i], n2_send.at[i], n2_recv.at[i], y_peers[i], band)
+
+    for i in range(7):
         n2(i).start()
 
-    acc = M0[...]
     for i in range(3):
-        x1(i).wait_recv()
-        acc = acc + X1[i].astype(f32)
-    SF[...] = acc
-    SB[...] = acc.astype(bf16)
+        for h in range(N_ZH):
+            x1(i, h).wait_recv()
+    for h in range(N_ZH):
+        acc = M0[h]
+        for i in range(3):
+            acc = acc + X1[i * N_ZH + h].astype(f32)
+        for y in range(N_Y):
+            to = y * 32 + h * 16
+            SF[to : to + 16, :] = acc[y * 16 : y * 16 + 16]
+            SB[to : to + 16, :] = acc[y * 16 : y * 16 + 16].astype(bf16)
 
     def x2(i):
-        a, b = yz_off[i]
-        row = (((zh + a) % N_ZH) * N_Y + (gy + b) % N_Y) * 16
+        row = ((gy + 1 + i) % N_Y) * 32
         return remote(
-            SB.at[pl.ds(pl.multiple_of(row, 16), 16)], X2.at[i], x2_send.at[i], x2_recv.at[i],
-            yz_peers[i], band,
+            SB.at[pl.ds(pl.multiple_of(row, 32), 32)], X2.at[i], x2_send.at[i], x2_recv.at[i],
+            y_peers[i], band,
         )
 
-    for i in range(15):
+    for i in (3, 2, 4, 1, 5, 0, 6):
         x2(i).start()
 
     total = N2s[...]
-    for i in range(15):
+    for i in range(7):
         n2(i).wait_recv()
         total = total + N2r[i]
-    inverse = lax.rsqrt(total[0:1, :] + epsilon)
-    OUT[...] = (CO[...] * inverse)[0:OWNED].astype(bf16)
+    N3s[...] = total
+    n3 = remote(N3s, N3r, n3_sem.at[0], n3_sem.at[1], z_peer, band)
+    n3.start()
+
+    m = SF[pl.ds(pl.multiple_of(gy * 32, 32), 32), :]
+    for i in range(7):
+        x2(i).wait_recv()
+        m = m + X2[i].astype(f32)
+    SZ[...] = m
+    x3 = remote(
+        SZ.at[pl.ds(pl.multiple_of((1 - zh) * 16, 16), 16)], X3, x3_sem.at[0], x3_sem.at[1], z_peer, band
+    )
+    x3.start()
+
+    n3.wait_recv()
+    inverse = lax.rsqrt((N3s[...] + N3r[...])[0:1, :] + epsilon)
+    OUT[...] = ((CO[:, 0:128] + CO[:, 128:256]) * inverse)[0:OWNED].astype(bf16)
     out_copy = pltpu.make_async_copy(OUT, out_ref, out_sem.at[0])
     out_copy.start()
-
-    m = SF[pl.ds(pl.multiple_of((zh * N_Y + gy) * 16, 16), 16), :]
-    for i in range(15):
-        x2(i).wait_recv()
-        m = m + X2[i].astype(f32)
-    margin_ref[...] = m * inverse
+    x3.wait_recv()
+    margin_ref[...] = (SZ[pl.ds(pl.multiple_of(zh * 16, 16), 16), :] + X3[...]) * inverse
     out_copy.wait()
+    n3.wait_send()
+    x3.wait_send()
 
     @pl.when(has_below)
     def _():
@@ -866,8 +909,9 @@
         forward(dist, False)
     for i in range(3):
         n1(i).wait_send()
-        x1(i).wait_send()
-    for i in range(15):
+        for h in range(N_ZH):
+            x1(i, h).wait_send()
+    for i in range(7):
         n2(i).wait_send()
         x2(i).wait_send()
 
@@ -918,6 +962,8 @@
         vm((4, MR, PLP), bf16),
         vm((PLP, PLP), bf16),
         vm((2, PLP, PLP), bf16),
+        vm((PLP, PLP), bf16),
+        vm((2, PLP, PLP), bf16),
         vm((2, PL, ORB), f32),
         vm((PL, ORB), f32),
         vm((DEGREE, PL, ORB), bf16),
@@ -933,19 +979,23 @@
         vm((8, OWNP, ORB), bf16),
         vm((NRL, 256), bf16),
         vm((OWNP, ORB), bf16),
-        vm((OWNP, ORB), f32),
-        vm((3, 256, ORB), bf16),
-        vm((3, 256, ORB), bf16),
-        vm((256, ORB), f32),
+        vm((OWNP, 256), f32),
+        vm((6, 128, ORB), bf16),
+        vm((6, 128, ORB), bf16),
+        vm((2, 128, ORB), f32),
         vm((256, ORB), f32),
         vm((256, ORB), bf16),
-        vm((15, 16, ORB), bf16),
+        vm((7, 32, ORB), bf16),
+        vm((32, ORB), f32),
+        vm((16, ORB), f32),
         vm((8, ORB), f32),
         vm((3, 8, ORB), f32),
         vm((8, ORB), f32),
-        vm((15, 8, ORB), f32),
+        vm((7, 8, ORB), f32),
+        vm((8, ORB), f32),
+        vm((8, ORB), f32),
         dma(8), dma(8), dma(8), dma(8), dma(2), dma(2), dma(20), dma(8),
-        dma(3), dma(3), dma(15), dma(15), dma(3), dma(3), dma(15), dma(15), dma(8), dma(1),
+        dma(6), dma(6), dma(7), dma(7), dma(3), dma(3), dma(7), dma(7), dma(2), dma(2), dma(8), dma(1),
     ]
     return pl.pallas_call(
         kernel,

time: 81.3 us -> 76.7 us (0.943)
  Pallas kernels: 78.2 us -> 73.6 us
    pallas_call x1, Pallas kernels: 78.2 us -> 73.6 us  [per_device(): pl.pallas_call(kernel, out_shape=(jax.ShapeDtypeStruct((OWNED, ORB), bf16...]
where the time goes in v4:
time: 76.7 us; the launch traced here: 76.5 us
  Pallas kernels  73.6 us (96%)
  local copies, waits for them, and re-layouts  2.27 us (3%)
    pallas_call x1, Pallas kernels, per_device(): pl.pallas_call(kernel, out_shape=(jax.ShapeDtypeStruct((OWNED, ORB), bf16...  73.6 us
    unnamed x4, local copies, waits for them, and re-layouts  2.27 us

profile of v4, /device:TPU:6, one launch (start us, length us, event | category | flops | bytes accessed | tf_op | source)
XLA Modules:
  0.0 76.5 jit_solution(8695675705282125851)
XLA Ops:
  0.6 73.6 %shard_map.86 = (bf16[1014,128]{1,0:T(8,128)(2,1)}, f32[16,128]{1,0:T(8,128)}) custom-call(bf16[1014,128]{1,0:T(8,128)(2,1)} %start_hbm.1, bf16[1014,128]{1,0:T(8,128)(2,1)} %res_hbm.1, bf16[343,343]{1,0:T(8,128)(2,1)} %ck_hbm.1, f32[4]{0:T(128)} %scale_hbm.1, f32[1,1014]{1,0:T(1,128)} %bitcast.2, s32[4,343]{1,0:T(4,128)} %cn_hbm.1, s32[1,169]{1,0:T(1,128)} %bitcast.3), custom_call_target="tpu_custom_call" | custom-call | flops 4000000000 | bytes 1000000 | tf_op jit(solution)/shard_map/pallas_call | solution.py:1000
  74.3 0.0 copy-start
  74.3 1.7 %copy.11 = bf16[1014,128]{1,0:T(8,128)(2,1)} copy(bf16[1014,128]{1,0:T(8,128)(2,1)} %get-tuple-element.4) | data formatting | bytes 519168
  75.9 0.0 copy-done
  75.9 0.6 copy.12
Async XLA Ops:
  74.3 1.7 %copy-start = (f32[16,128]{1,0:T(8,128)S(1)}, f32[16,128]{1,0:T(8,128)}, u32[]{:S(2)}) copy-start(f32[16,128]{1,0:T(8,128)} %get-tuple-element.5) | copy-start | bytes 24580

commit v5 on v4

--- a/solution.py
+++ b/solution.py
@@ -89,9 +89,9 @@
     start_ref, res_ref, ck_ref, scale_ref, pot_ref, cn_ref, cns_ref, sr_ref, OUT,
     V, R, O, OG, part, potc, place, prow, Pm, PT, Q, st, kpad, K1, Kp, T, KgP, KttP, KgD,
     ET, F, W2, top_col, jbot_col, pot8, cnp, srp,
-    RBT, R2, KgB, M1, WT, M1T, D2, CR, CR2, Ps, Qs, Gs, cs, Gr, cr, Js, Jr, Us, Ur, RB, H2, LOW, CO, mpb, X1, M0, SF, SB, X2, SZ, X3, N1s, N1r, N2s, N2r, N3s, N3r,
+    RBT, R2, KgB, M1, WT, M1T, D2, CR, CR2, Ps, Qs, Gs, cs, Gr, cr, Js, Jr, Us, Ur, RB, H2, LOW, CO, mpb, X1, M0, SF, SB, X2, N1s, N1r, N2s, N2r,
     g_send, g_recv, c_send, c_recv, j_sem, u_sem, r_send, r_recv, x1_send, x1_recv, x2_send, x2_recv,
-    n1_send, n1_recv, n2_send, n2_recv, n3_sem, x3_sem, in_sem, out_sem,
+    n1_send, n1_recv, n2_send, n2_recv, hello, in_sem, out_sem,
 ):
     d = lax.axis_index("domain")
     band = lax.axis_index("band")
@@ -453,6 +453,9 @@
     )
     pl.semaphore_wait(barrier, count)
 
+    for p in y_peers:
+        pl.semaphore_signal(hello, inc=1, device_id=(p, band), device_id_type=MESH)
+
     @pl.when(has_below)
     def _():
         j_copy.start()
@@ -827,10 +830,20 @@
         n1(i).wait_recv()
     N2s[...] = N1s[...] + N1r[0] + N1r[1] + N1r[2]
 
+    yz_off = [(a, b) for a in range(N_ZH) for b in range(N_Y) if (a, b) != (0, 0)]
+    far_first = sorted(range(15), key=lambda i: (-yz_off[i][0], abs(yz_off[i][1] - 4)))
+
+    def to_yz(i):
+        return (zh + yz_off[i][0]) % N_ZH, (gy + yz_off[i][1]) % N_Y
+
     def n2(i):
-        return remote(N2s, N2r.at[i], n2_send.at[i], n2_recv.at[i], y_peers[i], band)
-
-    for i in range(7):
+        to_z, to_y = to_yz(i)
+        return remote(
+            N2s, N2r.at[i], n2_send.at[i], n2_recv.at[i], (to_z * N_X + gx) * N_Y + to_y, band
+        )
+
+    pl.semaphore_wait(hello, len(y_peers))
+    for i in far_first:
         n2(i).start()
 
     for i in range(3):
@@ -846,43 +859,30 @@
             SB[to : to + 16, :] = acc[y * 16 : y * 16 + 16].astype(bf16)
 
     def x2(i):
-        row = ((gy + 1 + i) % N_Y) * 32
+        to_z, to_y = to_yz(i)
         return remote(
-            SB.at[pl.ds(pl.multiple_of(row, 32), 32)], X2.at[i], x2_send.at[i], x2_recv.at[i],
-            y_peers[i], band,
+            SB.at[pl.ds(pl.multiple_of(to_y * 32 + to_z * 16, 16), 16)], X2.at[i], x2_send.at[i],
+            x2_recv.at[i], (to_z * N_X + gx) * N_Y + to_y, band,
         )
 
-    for i in (3, 2, 4, 1, 5, 0, 6):
+    for i in far_first:
         x2(i).start()
 
     total = N2s[...]
-    for i in range(7):
+    for i in range(15):
         n2(i).wait_recv()
         total = total + N2r[i]
-    N3s[...] = total
-    n3 = remote(N3s, N3r, n3_sem.at[0], n3_sem.at[1], z_peer, band)
-    n3.start()
-
-    m = SF[pl.ds(pl.multiple_of(gy * 32, 32), 32), :]
-    for i in range(7):
-        x2(i).wait_recv()
-        m = m + X2[i].astype(f32)
-    SZ[...] = m
-    x3 = remote(
-        SZ.at[pl.ds(pl.multiple_of((1 - zh) * 16, 16), 16)], X3, x3_sem.at[0], x3_sem.at[1], z_peer, band
-    )
-    x3.start()
-
-    n3.wait_recv()
-    inverse = lax.rsqrt((N3s[...] + N3r[...])[0:1, :] + epsilon)
+    inverse = lax.rsqrt(total[0:1, :] + epsilon)
     OUT[...] = ((CO[:, 0:128] + CO[:, 128:256]) * inverse)[0:OWNED].astype(bf16)
     out_copy = pltpu.make_async_copy(OUT, out_ref, out_sem.at[0])
     out_copy.start()
-    x3.wait_recv()
-    margin_ref[...] = (SZ[pl.ds(pl.multiple_of(zh * 16, 16), 16), :] + X3[...]) * inverse
+
+    m = SF[pl.ds(pl.multiple_of(gy * 32 + zh * 16, 16), 16), :]
+    for i in range(15):
+        x2(i).wait_recv()
+        m = m + X2[i].astype(f32)
+    margin_ref[...] = m * inverse
     out_copy.wait()
-    n3.wait_send()
-    x3.wait_send()
 
     @pl.when(has_below)
     def _():
@@ -911,7 +911,7 @@
         n1(i).wait_send()
         for h in range(N_ZH):
             x1(i, h).wait_send()
-    for i in range(7):
+    for i in range(15):
         n2(i).wait_send()
         x2(i).wait_send()
 
@@ -985,17 +985,14 @@
         vm((2, 128, ORB), f32),
         vm((256, ORB), f32),
         vm((256, ORB), bf16),
-        vm((7, 32, ORB), bf16),
-        vm((32, ORB), f32),
-        vm((16, ORB), f32),
+        vm((15, 16, ORB), bf16),
         vm((8, ORB), f32),
         vm((3, 8, ORB), f32),
         vm((8, ORB), f32),
-        vm((7, 8, ORB), f32),
-        vm((8, ORB), f32),
-        vm((8, ORB), f32),
+        vm((15, 8, ORB), f32),
         dma(8), dma(8), dma(8), dma(8), dma(2), dma(2), dma(20), dma(8),
-        dma(6), dma(6), dma(7), dma(7), dma(3), dma(3), dma(7), dma(7), dma(2), dma(2), dma(8), dma(1),
+        dma(6), dma(6), dma(15), dma(15), dma(3), dma(3), dma(15), dma(15),
+        pltpu.SemaphoreType.REGULAR, dma(8), dma(1),
     ]
     return pl.pallas_call(
         kernel,

time: 76.7 us -> 74.7 us (0.974)
  Pallas kernels: 73.6 us -> 71.6 us
    pallas_call x1, Pallas kernels: 73.6 us -> 71.6 us  [per_device(): pl.pallas_call(kernel, out_shape=(jax.ShapeDtypeStruct((OWNED, ORB), bf16...]
where the time goes in v5:
time: 74.7 us; the launch traced here: 74.5 us
  Pallas kernels  71.6 us (96%)
  local copies, waits for them, and re-layouts  2.27 us (3%)
    pallas_call x1, Pallas kernels, per_device(): pl.pallas_call(kernel, out_shape=(jax.ShapeDtypeStruct((OWNED, ORB), bf16...  71.6 us
    unnamed x4, local copies, waits for them, and re-layouts  2.27 us

profile of v5, /device:TPU:6, one launch (start us, length us, event | category | flops | bytes accessed | tf_op | source)
XLA Modules:
  0.0 74.5 jit_solution(6416957740158408741)
XLA Ops:
  0.6 71.6 %shard_map.86 = (bf16[1014,128]{1,0:T(8,128)(2,1)}, f32[16,128]{1,0:T(8,128)}) custom-call(bf16[1014,128]{1,0:T(8,128)(2,1)} %start_hbm.1, bf16[1014,128]{1,0:T(8,128)(2,1)} %res_hbm.1, bf16[343,343]{1,0:T(8,128)(2,1)} %ck_hbm.1, f32[4]{0:T(128)} %scale_hbm.1, f32[1,1014]{1,0:T(1,128)} %bitcast.2, s32[4,343]{1,0:T(4,128)} %cn_hbm.1, s32[1,169]{1,0:T(1,128)} %bitcast.3), custom_call_target="tpu_custom_call" | custom-call | flops 4000000000 | bytes 1000000 | tf_op jit(solution)/shard_map/pallas_call | solution.py:997
  72.2 0.0 copy-start
  72.2 1.7 %copy.11 = bf16[1014,128]{1,0:T(8,128)(2,1)} copy(bf16[1014,128]{1,0:T(8,128)(2,1)} %get-tuple-element.4) | data formatting | bytes 519168
  73.9 0.0 copy-done
  73.9 0.6 copy.12
Async XLA Ops:
  72.2 1.7 %copy-start = (f32[16,128]{1,0:T(8,128)S(1)}, f32[16,128]{1,0:T(8,128)}, u32[]{:S(2)}) copy-start(f32[16,128]{1,0:T(8,128)} %get-tuple-element.5) | copy-start | bytes 24580

commit v6 on v5

--- a/solution.py
+++ b/solution.py
@@ -437,11 +437,14 @@
 
         for X in range(NX):
             to_operand(R, X, V[cur, X * XS : X * XS + 104, :])
-        prepare_up(k)
-
-        @pl.when(has_above & jnp.logical_not(up_early))
-        def _():
-            up(k, cs).start()
+
+        @pl.when(jnp.logical_not(up_early))
+        def _():
+            prepare_up(k)
+
+            @pl.when(has_above)
+            def _():
+                up(k, cs).start()
 
     prepare_down(0, 0)
     prepare_up(0)
@@ -786,6 +789,10 @@
         send_planes(k + 1, 1 - cur)
         bulk(k + 1, 1 - cur)
         early_up(k + 1)
+
+        @pl.when(up_early)
+        def _():
+            prepare_up(k + 1)
 
         @pl.when(down_early & (k + 1 < DEGREE - 1))
         def _():

time: 74.7 us -> 74.4 us (level)
  no operation moved by 1% of the time
where the time goes in v6:
time: 74.4 us; the launch traced here: 74.1 us
  Pallas kernels  71.1 us (96%)
  local copies, waits for them, and re-layouts  2.27 us (3%)
    pallas_call x1, Pallas kernels, per_device(): pl.pallas_call(kernel, out_shape=(jax.ShapeDtypeStruct((OWNED, ORB), bf16...  71.1 us
    unnamed x4, local copies, waits for them, and re-layouts  2.27 us

profile of v6, /device:TPU:6, one launch (start us, length us, event | category | flops | bytes accessed | tf_op | source)
XLA Modules:
  0.0 74.1 jit_solution(3820449542274091868)
XLA Ops:
  0.6 71.1 %shard_map.86 = (bf16[1014,128]{1,0:T(8,128)(2,1)}, f32[16,128]{1,0:T(8,128)}) custom-call(bf16[1014,128]{1,0:T(8,128)(2,1)} %start_hbm.1, bf16[1014,128]{1,0:T(8,128)(2,1)} %res_hbm.1, bf16[343,343]{1,0:T(8,128)(2,1)} %ck_hbm.1, f32[4]{0:T(128)} %scale_hbm.1, f32[1,1014]{1,0:T(1,128)} %bitcast.2, s32[4,343]{1,0:T(4,128)} %cn_hbm.1, s32[1,169]{1,0:T(1,128)} %bitcast.3), custom_call_target="tpu_custom_call" | custom-call | flops 4000000000 | bytes 1000000 | tf_op jit(solution)/shard_map/pallas_call | solution.py:1004
  71.8 0.0 copy-start
  71.8 1.7 %copy.11 = bf16[1014,128]{1,0:T(8,128)(2,1)} copy(bf16[1014,128]{1,0:T(8,128)(2,1)} %get-tuple-element.4) | data formatting | bytes 519168
  73.5 0.0 copy-done
  73.5 0.6 copy.12
Async XLA Ops:
  71.8 1.7 %copy-start = (f32[16,128]{1,0:T(8,128)S(1)}, f32[16,128]{1,0:T(8,128)}, u32[]{:S(2)}) copy-start(f32[16,128]{1,0:T(8,128)} %get-tuple-element.5) | copy-start | bytes 24580
